TPU v7x, 32 devices: a whole 2x2x4 slice. The times are simulated.
32 devices in a mesh: clip: 8 (over y, x, core), frame: 4 (over z).
Axes of the slice: x: 2, y: 2, z: 4, core: 2. Of those that a mesh axis runs over, the one named last changes fastest.
Arguments:
- inputs: bfloat16 [16, 16, 256, 768], P('clip', 'frame'), may hold values from -6 to 6
- cotangent: bfloat16 [16, 16, 256, 768], P('clip', 'frame'), may hold values from -6 to 6
- time_steps: int32 [16], P('clip'), may hold values from 0 to 999
- weight_index: int32 [16], P('clip'), may hold values from 0 to 7
- ada_weight: bfloat16 [768, 6912], P(('clip', 'frame')), may hold values from -0.4375 to 0.4375
- ada_bias: bfloat16 [6912], P(('clip', 'frame')), may hold values from -2.390625 to 2.390625
- space_qkv: bfloat16 [768, 2304], P(('clip', 'frame')), may hold values from -0.21875 to 0.21875
- space_out: bfloat16 [768, 768], P(('clip', 'frame')), may hold values from -0.875 to 0.875
- space_out_bias: bfloat16 [768], P(('clip', 'frame')), may hold values from -3 to 3
- time_qkv: bfloat16 [768, 2304], P(('clip', 'frame')), may hold values from -0.21875 to 0.21875
- time_out: bfloat16 [768, 768], P(('clip', 'frame')), may hold values from -0.4375 to 0.4375
- time_out_bias: bfloat16 [768], P(('clip', 'frame')), may hold values from -3 to 3
- up_weight: bfloat16 [768, 3072], P(('clip', 'frame')), may hold values from -0.21875 to 0.21875
- up_bias: bfloat16 [3072], P(('clip', 'frame')), may hold values from -3 to 3
- down_weight: bfloat16 [3072, 768], P(('clip', 'frame')), may hold values from -0.109375 to 0.109375
- down_bias: bfloat16 [768], P(('clip', 'frame')), may hold values from -3 to 3
Outputs:
- block_output: bfloat16 [16, 16, 256, 768], P('clip', 'frame')
- input_grad: float32 [16, 16, 256, 768], P('clip', 'frame')
- grad_ada_weight: float32 [768, 6912], P(('clip', 'frame'))
- grad_ada_bias: float32 [6912], P(('clip', 'frame'))
- grad_space_qkv: float32 [768, 2304], P(('clip', 'frame'))
- grad_space_out: float32 [768, 768], P(('clip', 'frame'))
- grad_space_out_bias: float32 [768], P(('clip', 'frame'))
- grad_time_qkv: float32 [768, 2304], P(('clip', 'frame'))
- grad_time_out: float32 [768, 768], P(('clip', 'frame'))
- grad_time_out_bias: float32 [768], P(('clip', 'frame'))
- grad_up_weight: float32 [768, 3072], P(('clip', 'frame'))
- grad_up_bias: float32 [3072], P(('clip', 'frame'))
- grad_down_weight: float32 [3072, 768], P(('clip', 'frame'))
- grad_down_bias: float32 [768], P(('clip', 'frame'))
All inputs are finite; a program needn't handle non-finite values.
Results may differ from a plain program's by a relative error of at most 0.02.
Values may be sent and summed in bfloat16 or wider, within the bound.
A program may use at most 320 MiB of HBM per device.

v0:
```python
import math

import jax
import jax.numpy as jnp
from jax import lax
from jax.sharding import PartitionSpec as P

HEADS = 12
HEAD = 64


highest = lax.Precision.HIGHEST


def embed_steps(time_steps, model_width):
    half_width = model_width // 2
    frequencies = jnp.exp(
        -math.log(10000.0) * jnp.arange(half_width, dtype=jnp.float32) / half_width
    )
    angles = time_steps.astype(jnp.float32)[:, None] * frequencies[None, :]
    return jnp.concatenate([jnp.cos(angles), jnp.sin(angles)], axis=1)


def modulated_norm(values, scaling, offset):
    centred = values - jnp.mean(values, axis=-1, keepdims=True)
    variance = jnp.mean(centred * centred, axis=-1, keepdims=True)
    return centred * lax.rsqrt(variance + 1e-06) * (1.0 + scaling) + offset


def gelu_tanh(values):
    return jax.nn.gelu(values, approximate=True)


def attend(queries, keys_all, values_all):
    scores = (
        jnp.einsum("abihe,abjhe->abhij", queries, keys_all, preferred_element_type=jnp.float32)
        * 0.125
    )
    row_peak = jnp.max(scores, axis=-1, keepdims=True)
    terms = jnp.exp(scores - row_peak)
    row_totals = jnp.sum(terms, axis=-1, keepdims=True)
    attention = (terms / row_totals).astype(jnp.bfloat16)
    mixed = jnp.einsum(
        "abhij,abjhe->abihe", attention, values_all, preferred_element_type=jnp.float32
    )
    return (mixed.astype(jnp.bfloat16), row_peak + jnp.log(row_totals))


def attend_back(queries, keys_all, values_all, log_totals, grad_mixed):
    scores = (
        jnp.einsum("abihe,abjhe->abhij", queries, keys_all, preferred_element_type=jnp.float32)
        * 0.125
    )
    attention = jnp.exp(scores - log_totals)
    grad_attention = jnp.einsum(
        "abihe,abjhe->abhij", grad_mixed, values_all, preferred_element_type=jnp.float32
    )
    row_inner = jnp.sum(attention * grad_attention, axis=-1, keepdims=True)
    grad_scores = (attention * (grad_attention - row_inner)).astype(jnp.bfloat16)
    grad_queries = (
        jnp.einsum("abhij,abjhe->abihe", grad_scores, keys_all, preferred_element_type=jnp.float32)
        * 0.125
    )
    grad_keys = (
        jnp.einsum("abhij,abihe->abjhe", grad_scores, queries, preferred_element_type=jnp.float32)
        * 0.125
    )
    grad_values = jnp.einsum(
        "abhij,abihe->abjhe",
        attention.astype(jnp.bfloat16),
        grad_mixed,
        preferred_element_type=jnp.float32,
    )
    return jnp.stack([grad_queries, grad_keys, grad_values], axis=3)


def project(left, right):
    return jnp.einsum("cfpd,dk->cfpk", left, right, preferred_element_type=jnp.float32)


def project_back(left, right):
    return jnp.einsum("cfpk,dk->cfpd", left, right, preferred_element_type=jnp.float32)


def weight_term(left, right):
    return jnp.einsum("cfpd,cfpk->dk", left, right, preferred_element_type=jnp.float32)


def column_sums(values):
    return jnp.sum(values.astype(jnp.float32), axis=(0, 1, 2))


def clip_sums(values):
    return jnp.sum(values, axis=(1, 2))


def as_lanes(matrix):
    return matrix.reshape(-1, 128)


def own_slice(vector, owner, parts):
    length = vector.shape[0] // parts
    return lax.dynamic_slice_in_dim(vector, owner * length, length, 0)


def shards(
    inputs,
    cotangent,
    time_steps,
    weight_index,
    ada_weight,
    ada_bias,
    space_qkv,
    space_out,
    space_out_bias,
    time_qkv,
    time_out,
    time_out_bias,
    up_weight,
    up_bias,
    down_weight,
    down_bias,
):
    clip_count, frame_count, patch_count, model_width = inputs.shape
    owner = lax.axis_index(("clip", "frame"))
    owner_total = lax.axis_size(("clip", "frame"))
    gathered = (
        lax.all_gather(ada_weight, ("clip", "frame"), axis=0, tiled=True),
        lax.all_gather(ada_bias, ("clip", "frame"), axis=0, tiled=True),
        lax.all_gather(space_qkv, ("clip", "frame"), axis=0, tiled=True),
        lax.all_gather(space_out, ("clip", "frame"), axis=0, tiled=True),
        lax.all_gather(space_out_bias, ("clip", "frame"), axis=0, tiled=True),
        lax.all_gather(time_qkv, ("clip", "frame"), axis=0, tiled=True),
        lax.all_gather(time_out, ("clip", "frame"), axis=0, tiled=True),
        lax.all_gather(time_out_bias, ("clip", "frame"), axis=0, tiled=True),
        lax.all_gather(up_weight, ("clip", "frame"), axis=0, tiled=True),
        lax.all_gather(up_bias, ("clip", "frame"), axis=0, tiled=True),
        lax.all_gather(down_weight, ("clip", "frame"), axis=0, tiled=True),
        lax.all_gather(down_bias, ("clip", "frame"), axis=0, tiled=True),
    )
    w_ada, b_ada, w_sqkv, w_sout, b_sout, w_tqkv, w_tout, b_tout, w_up, b_up, w_down, b_down = (
        gathered
    )
    silu_embed = jax.nn.silu(embed_steps(time_steps, model_width)).astype(jnp.bfloat16)
    modulation = jnp.dot(silu_embed, w_ada, preferred_element_type=jnp.float32) + b_ada.astype(
        jnp.float32
    )
    residual = inputs.astype(jnp.float32)
    pieces = [
        modulation[:, None, None, number * model_width : (number + 1) * model_width]
        for number in range(9)
    ]
    normed_one, norm_back_one = jax.vjp(modulated_norm, residual, pieces[1], pieces[0])
    hidden_one = normed_one.astype(jnp.bfloat16)
    qkv_one = project(hidden_one, w_sqkv).astype(jnp.bfloat16)
    split_one = qkv_one.reshape(clip_count, frame_count, patch_count, 3, HEADS, HEAD)
    mixed_one, totals_one = attend(
        split_one[:, :, :, 0], split_one[:, :, :, 1], split_one[:, :, :, 2]
    )
    flat_one = mixed_one.reshape(clip_count, frame_count, patch_count, model_width)
    branch_one = project(flat_one, w_sout) + b_sout.astype(jnp.float32)
    after_one = residual + pieces[2] * branch_one
    normed_two, norm_back_two = jax.vjp(modulated_norm, after_one, pieces[4], pieces[3])
    hidden_two = normed_two.astype(jnp.bfloat16)
    patch_hidden = lax.all_to_all(hidden_two, "frame", split_axis=2, concat_axis=1, tiled=True)
    frames_all = patch_hidden.shape[1]
    patch_local = patch_hidden.shape[2]
    qkv_two = project(patch_hidden, w_tqkv).astype(jnp.bfloat16)
    split_two = jnp.swapaxes(
        qkv_two.reshape(clip_count, frames_all, patch_local, 3, HEADS, HEAD), 1, 2
    )
    mixed_two, totals_two = attend(
        split_two[:, :, :, 0], split_two[:, :, :, 1], split_two[:, :, :, 2]
    )
    patch_mixed = jnp.swapaxes(mixed_two, 1, 2).reshape(
        clip_count, frames_all, patch_local, model_width
    )
    flat_two = lax.all_to_all(patch_mixed, "frame", split_axis=1, concat_axis=2, tiled=True)
    branch_two = project(flat_two, w_tout) + b_tout.astype(jnp.float32)
    after_two = after_one + pieces[5] * branch_two
    normed_three, norm_back_three = jax.vjp(modulated_norm, after_two, pieces[7], pieces[6])
    hidden_three = normed_three.astype(jnp.bfloat16)
    upper = project(hidden_three, w_up) + b_up.astype(jnp.float32)
    activated, gelu_back = jax.vjp(gelu_tanh, upper)
    activated = activated.astype(jnp.bfloat16)
    branch_three = project(activated, w_down) + b_down.astype(jnp.float32)
    outputs = (after_two + pieces[8] * branch_three).astype(jnp.bfloat16)
    regathered = (
        lax.all_gather(space_qkv, ("clip", "frame"), axis=0, tiled=True),
        lax.all_gather(space_out, ("clip", "frame"), axis=0, tiled=True),
        lax.all_gather(time_qkv, ("clip", "frame"), axis=0, tiled=True),
        lax.all_gather(time_out, ("clip", "frame"), axis=0, tiled=True),
        lax.all_gather(up_weight, ("clip", "frame"), axis=0, tiled=True),
        lax.all_gather(down_weight, ("clip", "frame"), axis=0, tiled=True),
    )
    w_sqkv, w_sout, w_tqkv, w_tout, w_up, w_down = regathered
    loss_scale = jnp.exp2(weight_index.astype(jnp.float32) * 0.5 - 1.0)
    grad_out = cotangent.astype(jnp.float32) * loss_scale[:, None, None, None]
    grad_branch_three = (grad_out * pieces[8]).astype(jnp.bfloat16)
    grad_gate_three = clip_sums(grad_out * branch_three)
    grad_down = weight_term(activated, grad_branch_three)
    grad_down_bias = column_sums(grad_branch_three)
    grad_activated = project_back(grad_branch_three, w_down)
    (grad_upper,) = gelu_back(grad_activated)
    grad_upper = grad_upper.astype(jnp.bfloat16)
    grad_up = weight_term(hidden_three, grad_upper)
    grad_up_bias = column_sums(grad_upper)
    grad_hidden_three = project_back(grad_upper, w_up)
    grad_after_two, grad_scale_three, grad_shift_three = norm_back_three(grad_hidden_three)
    grad_after_two = grad_after_two + grad_out
    grad_branch_two = (grad_after_two * pieces[5]).astype(jnp.bfloat16)
    grad_gate_two = clip_sums(grad_after_two * branch_two)
    grad_tout = weight_term(flat_two, grad_branch_two)
    grad_tout_bias = column_sums(grad_branch_two)
    grad_flat_two = project_back(grad_branch_two, w_tout).astype(jnp.bfloat16)
    patch_grad = lax.all_to_all(grad_flat_two, "frame", split_axis=2, concat_axis=1, tiled=True)
    split_grad = jnp.swapaxes(
        patch_grad.reshape(clip_count, frames_all, patch_local, HEADS, HEAD), 1, 2
    )
    grad_split_two = attend_back(
        split_two[:, :, :, 0], split_two[:, :, :, 1], split_two[:, :, :, 2], totals_two, split_grad
    )
    grad_qkv_two = (
        jnp.swapaxes(grad_split_two, 1, 2)
        .reshape(clip_count, frames_all, patch_local, 3 * model_width)
        .astype(jnp.bfloat16)
    )
    grad_tqkv = weight_term(patch_hidden, grad_qkv_two)
    grad_patch_hidden = project_back(grad_qkv_two, w_tqkv).astype(jnp.bfloat16)
    grad_hidden_two = lax.all_to_all(
        grad_patch_hidden, "frame", split_axis=1, concat_axis=2, tiled=True
    ).astype(jnp.float32)
    grad_after_one, grad_scale_two, grad_shift_two = norm_back_two(grad_hidden_two)
    grad_after_one = grad_after_one + grad_after_two
    grad_branch_one = (grad_after_one * pieces[2]).astype(jnp.bfloat16)
    grad_gate_one = clip_sums(grad_after_one * branch_one)
    grad_sout = weight_term(flat_one, grad_branch_one)
    grad_sout_bias = column_sums(grad_branch_one)
    grad_flat_one = project_back(grad_branch_one, w_sout).astype(jnp.bfloat16)
    split_grad_one = grad_flat_one.reshape(clip_count, frame_count, patch_count, HEADS, HEAD)
    grad_split_one = attend_back(
        split_one[:, :, :, 0],
        split_one[:, :, :, 1],
        split_one[:, :, :, 2],
        totals_one,
        split_grad_one,
    )
    grad_qkv_one = grad_split_one.reshape(
        clip_count, frame_count, patch_count, 3 * model_width
    ).astype(jnp.bfloat16)
    grad_sqkv = weight_term(hidden_one, grad_qkv_one)
    grad_hidden_one = project_back(grad_qkv_one, w_sqkv)
    grad_inputs, grad_scale_one, grad_shift_one = norm_back_one(grad_hidden_one)
    grad_inputs = grad_inputs + grad_after_one
    members = (
        grad_shift_one,
        grad_scale_one,
        grad_gate_one,
        grad_shift_two,
        grad_scale_two,
        grad_gate_two,
        grad_shift_three,
        grad_scale_three,
        grad_gate_three,
    )
    grad_modulation = jnp.concatenate(
        [member.reshape(clip_count, model_width) for member in members], axis=1
    )
    shapes = (
        grad_sqkv.shape[1],
        grad_sout.shape[1],
        grad_tqkv.shape[1],
        grad_tout.shape[1],
        grad_up.shape[1],
        grad_down.shape[1],
    )
    grad_ada = jnp.dot(silu_embed.astype(jnp.float32).T, grad_modulation, precision=highest)
    grad_ada_bias = jnp.sum(grad_modulation, axis=0)
    owned = (
        lax.psum_scatter(as_lanes(grad_ada), ("clip", "frame"), scatter_dimension=0, tiled=True),
        lax.psum_scatter(as_lanes(grad_sqkv), ("clip", "frame"), scatter_dimension=0, tiled=True),
        lax.psum_scatter(as_lanes(grad_sout), ("clip", "frame"), scatter_dimension=0, tiled=True),
        lax.psum_scatter(as_lanes(grad_tqkv), ("clip", "frame"), scatter_dimension=0, tiled=True),
        lax.psum_scatter(as_lanes(grad_tout), ("clip", "frame"), scatter_dimension=0, tiled=True),
        lax.psum_scatter(as_lanes(grad_up), ("clip", "frame"), scatter_dimension=0, tiled=True),
        lax.psum_scatter(as_lanes(grad_down), ("clip", "frame"), scatter_dimension=0, tiled=True),
    )
    summed_biases = lax.psum(
        (grad_ada_bias, grad_sout_bias, grad_tout_bias, grad_up_bias, grad_down_bias),
        ("clip", "frame"),
    )
    own_ada = owned[0].reshape(-1, grad_ada.shape[1])
    own_ada_bias = own_slice(summed_biases[0], owner, owner_total)
    matrices = owned[1:]
    biases = summed_biases[1:]
    own_mats = [matrices[number].reshape(-1, shapes[number]) for number in range(6)]
    own_biases = [own_slice(biases[number], owner, owner_total) for number in range(4)]
    return (
        outputs,
        grad_inputs,
        own_ada,
        own_ada_bias,
        own_mats[0],
        own_mats[1],
        own_biases[0],
        own_mats[2],
        own_mats[3],
        own_biases[1],
        own_mats[4],
        own_biases[2],
        own_mats[5],
        own_biases[3],
    )


def solution(mesh):
    in_specs = (
        P("clip", "frame", None, None),
        P("clip", "frame", None, None),
        P("clip"),
        P("clip"),
        P(("clip", "frame"), None),
        P(("clip", "frame")),
        P(("clip", "frame"), None),
        P(("clip", "frame"), None),
        P(("clip", "frame")),
        P(("clip", "frame"), None),
        P(("clip", "frame"), None),
        P(("clip", "frame")),
        P(("clip", "frame"), None),
        P(("clip", "frame")),
        P(("clip", "frame"), None),
        P(("clip", "frame")),
    )
    out_specs = (
        P("clip", "frame", None, None),
        P("clip", "frame", None, None),
        P(("clip", "frame"), None),
        P(("clip", "frame")),
        P(("clip", "frame"), None),
        P(("clip", "frame"), None),
        P(("clip", "frame")),
        P(("clip", "frame"), None),
        P(("clip", "frame"), None),
        P(("clip", "frame")),
        P(("clip", "frame"), None),
        P(("clip", "frame")),
        P(("clip", "frame"), None),
        P(("clip", "frame")),
    )
    return jax.shard_map(shards, mesh=mesh, in_specs=in_specs, out_specs=out_specs, check_vma=False)
```

profile of v0, /device:TPU:0, one launch (start us, length us, event | category | flops | bytes accessed | tf_op | source)
XLA Modules:
  0.0 1660.8 jit_solution(10469958150536721335)
XLA Ops:
  17.9 43.5 %all-reduce.6 = (bf16[6912]{0:T(1024)(128)(2,1)S(1)}, bf16[768]{0:T(1024)(128)(2,1)S(1)}, bf16[768]{0:T(1024)(128)(2,1)}, bf16[3072]{0:T(1024)(128)(2,1)}, bf16[768]{0:T(1024)(128)(2,1)}) all-reduce(bf16[6912]{0:T(1024)(128)(2,1)S(1)} %dynamic-update-slice, ...), channel_id=1, replica_groups=mesh['clip'=8,'frame'=4] {'clip','frame'}, use_global_device_ids=true, to_apply=%add | all-reduce | flops 12288 | bytes 49152
  61.6 39.4 %all-gather.8.cloned.1.call-done = bf16[768,6912]{1,0:T(8,128)(2,1)} async-done(((bf16[24,6912]{1,0:T(8,128)(2,1)}), bf16[768,6912]{1,0:T(8,128)(2,1)}) %all-gather.8.cloned.1.call-update) | async-done | bytes 10616848 | tf_op jit(solution)/shard_map/all_gather | solution.py:128
  107.3 55.1 %all-gather.10.cloned.1.call-done = bf16[768,2304]{1,0:T(8,128)(2,1)} async-done(((bf16[24,2304]{1,0:T(8,128)(2,1)}), bf16[768,2304]{1,0:T(8,128)(2,1)}) %all-gather.10.cloned.1.call-update) | async-done | bytes 3538960 | tf_op jit(solution)/shard_map/all_gather | solution.py:130
  174.8 12.6 copy.108
  187.4 14.7 multiply_reduce_fusion.1
  213.5 13.8 fusion.70
  248.4 82.7 %all-to-all-done = bf16[2,4,256,768]{3,1,0,2:T(4,128)(2,1)S(1)} async-done(((bf16[2,4,256,768]{3,1,0,2:T(4,128)(2,1)}), bf16[2,4,256,768]{3,1,0,2:T(4,128)(2,1)S(1)}, u32[]{:S(2)}, u32[]{:S(2)}) %all-to-all-start) | async-done | bytes 3145760 | tf_op jit(solution)/shard_map/all_to_all | solution.py:165
  333.5 12.7 convolution_convert_fusion
  346.2 28.7 %reshape.219 = bf16[2,16,64,3,12,64]{5,4,3,2,1,0:T(8,128)(2,1)} reshape(bf16[2,16,64,2304]{3,2,1,0:T(8,128)(2,1)} %convolution_convert_fusion) | data formatting | bytes 18874368 | tf_op jit(solution)/shard_map/reshape | solution.py:170
  375.0 20.2 %copy.185 = bf16[2,16,64,3,12,64]{5,1,4,2,0,3:T(8,128)(2,1)} copy(bf16[2,16,64,3,12,64]{5,4,3,2,1,0:T(8,128)(2,1)} %reshape.219) | data formatting | bytes 18874368 | tf_op jit(solution)/shard_map/reshape | solution.py:170
  451.3 78.2 %all-to-all-done.1 = bf16[2,16,64,768]{3,2,0,1:T(8,128)(2,1)S(1)} async-done(((bf16[2,16,64,768]{3,2,0,1:T(8,128)(2,1)}), bf16[2,16,64,768]{3,2,0,1:T(8,128)(2,1)S(1)}, u32[]{:S(2)}, u32[]{:S(2)}) %all-to-all-start.1) | async-done | bytes 3145760 | tf_op jit(solution)/shard_map/all_to_all | solution.py:178
  545.0 24.7 %multiply_convert_fusion.1 = (bf16[2,4,256,3072]{3,2,1,0:T(8,128)(2,1)}, f32[2,4,256,3072]{3,2,1,0:T(8,128)}) fusion(f32[3072]{0:T(1024)S(1)} %convert_element_type.165, bf16[768,3072]{1,0:T(8,128)(2,1)} %all-gather.18.cloned.1.call-done, f32[2,4,256,768]{3,2,1,0:T(8,128)} %copy-done.2, f32[2,768]{1,0:T(2,128)S(1)} %copy-done.58, ...), kind=kOutput, calls=%fused_computation.14 | convolution fusion | flops 9734455296 | bytes 48799744 | tf_op jit(solution)/shard_map/cfpd,dk->cfpk/dot_general | solution.py:78
  569.7 34.4 %convert_reduce_fusion = (f32[3072]{0:T(1024)}, bf16[2,4,256,3072]{3,2,1,0:T(8,128)(2,1)}) fusion(f32[2,4,256,3072]{3,2,1,0:T(8,128)} %get-tuple-element.69, f32[3072]{0:T(1024)S(1)} %convert_element_type.165, bf16[3072,768]{1,0:T(8,128)(2,1)} %all-gather.20.cloned.1.call-done, bf16[2,4,256,768]{3,2,1,0:T(8,128)(2,1)} %param.17, ...), kind=kOutput, calls=%fused_computation.10 | convolution fusion | flops 9814668288 | bytes 45643784 | tf_op jit(solution)/shard_map/cfpk,dk->cfpd/dot_general | solution.py:82
  604.2 15.3 multiply_reduce_fusion.9
  623.5 21.7 %convert_reduce_fusion.2 = (f32[768]{0:T(1024)}, f32[2,768]{1,0:T(2,128)}, bf16[2,4,256,768]{3,2,1,0:T(8,128)(2,1)}, f32[768]{0:T(1024)}, bf16[2,4,256,768]{3,2,1,0:T(8,128)(2,1)}, /*index=5*/f32[2,4,256,768]{3,2,1,0:T(8,128)}) fusion(f32[2,768]{1,0:T(2,128)S(1)} %copy-done.57, f32[2]{0:T(128)S(1)} %multiply_exponential_fusion.1, ...), kind=kOutput, calls=%fused_computation.67 | convolution fusion | flops 9701422080 | bytes 45679624 | tf_op jit(solution)/shard_map/cfpd,dk->cfpk/dot_general | solution.py:78
  652.4 18.2 %convolution_bitcast_fusion.3 = f32[768,3072]{1,0:T(8,128)} fusion(bf16[2,4,256,3072]{3,2,1,0:T(8,128)(2,1)} %get-tuple-element.79, f32[2,4,256,768]{3,2,1,0:T(8,128)} %copy-done.2, f32[2,768]{1,0:T(2,128)S(1)} %copy-done.58, f32[2,768]{1,0:T(2,128)S(1)} %copy-done.45, f32[2,4,256]{2,1,0:T(4,128)S(1)} %fusion.85, f32[2,4,256]{2,1,0:T(4,128)S(1)} %broadcast_multiply_fusion), kind=kOutput, calls=%fused_computation.98 | convolution fusion | flops 9671540736 | bytes 28340224 | tf_op jit(solution)/shard_map/cfpd,cfpk->dk/dot_general | solution.py:86
  696.4 17.1 %convolution_bitcast_fusion = f32[3072,768]{1,0:T(8,128)} fusion(bf16[2,4,256,3072]{3,2,1,0:T(8,128)(2,1)} %get-tuple-element.68, bf16[2,4,256,768]{3,2,1,0:T(8,128)(2,1)} %param.17, f32[2]{0:T(128)S(1)} %multiply_exponential_fusion.1, f32[2,768]{1,0:T(2,128)S(1)} %copy-done.57), kind=kOutput, calls=%fused_computation.95 | convolution fusion | flops 9669967872 | bytes 25171976 | tf_op jit(solution)/shard_map/cfpd,cfpk->dk/dot_general | solution.py:86
  724.3 52.9 %all-to-all-done.2 = bf16[2,4,256,768]{3,1,0,2:T(4,128)(2,1)} async-done(((bf16[2,4,256,768]{3,1,0,2:T(4,128)(2,1)}), bf16[2,4,256,768]{3,1,0,2:T(4,128)(2,1)}, u32[]{:S(2)}, u32[]{:S(2)}) %all-to-all-start.2) | async-done | bytes 3145760 | tf_op jit(solution)/shard_map/all_to_all | solution.py:216
  792.1 16.4 multiply_reduce_fusion.2
  808.4 14.0 multiply_convert_fusion.2
  862.9 15.0 copy.126
  877.9 30.4 %convert_element_type.179 = bf16[2,16,64,2304]{3,2,1,0:T(8,128)(2,1)} reshape(bf16[2,16,64,3,12,64]{5,4,3,2,1,0:T(8,128)(2,1)} %copy.126) | data formatting | bytes 18874368 | tf_op jit(solution)/shard_map/convert_element_type | solution.py:226
  918.8 93.3 %all_to_all.60 = bf16[2,16,64,768]{3,2,0,1:T(8,128)(2,1)S(1)} all-to-all(bf16[2,16,64,768]{3,2,0,1:T(8,128)(2,1)S(1)} %copy.127), channel_id=1, replica_groups=mesh['clip'=8,'frame'=4] {'frame'}, dimensions={1} | all-to-all | bytes 6291456 | tf_op jit(solution)/shard_map/all_to_all | solution.py:230
  1041.7 12.7 convolution_bitcast_fusion.1
  1073.2 19.1 %multiply_reduce_fusion = (f32[2,4,12,256]{3,2,1,0:T(8,128)S(1)}, f32[2,4,12,256,256]{3,4,2,1,0:T(8,128)}) fusion(f32[2,4,12,256,256]{3,4,2,1,0:T(8,128)} %get-tuple-element.63, f32[2,4,12,256]{3,2,1,0:T(8,128)S(1)} %log_add_fusion.1, bf16[2,4,256,12,64]{2,4,3,1,0:T(8,128)(2,1)S(1)} %bitcast.260, bf16[2,4,256,3,12,64]{2,5,4,3,1,0:T(8,128)(2,1)} %bitcast.255), kind=kOutput, calls=%fused_computation.12 | convolution fusion | flops 830447616 | bytes 56819712 | tf_op jit(solution)/shard_map/abihe,abjhe->abhij/dot_general | solution.py:55
  1092.3 22.4 %multiply_convert_fusion = bf16[2,4,12,256,256]{3,4,2,1,0:T(8,128)(2,1)} fusion(f32[2,4,12,256,256]{3,4,2,1,0:T(8,128)} %get-tuple-element.75, f32[2,4,12,256,256]{3,4,2,1,0:T(8,128)} %get-tuple-element.63, f32[2,4,12,256]{3,2,1,0:T(8,128)S(1)} %get-tuple-element.74, f32[2,4,12,256]{3,2,1,0:T(8,128)S(1)} %log_add_fusion.1), kind=kLoop, calls=%fused_computation.11 | loop fusion | flops 31457280 | bytes 63111168 | tf_op jit(solution)/shard_map/convert_element_type | solution.py:59
  1135.7 14.5 convert_bitcast_fusion.1
  1168.1 14.5 convolution_bitcast_fusion.2
  1227.6 22.2 %reshape.223 = f32[41472,128]{1,0:T(8,128)} reshape(f32[768,6912]{1,0:T(8,128)} %fusion.91) | data formatting | bytes 42467328 | tf_op jit(solution)/shard_map/reshape | solution.py:98
  1251.6 39.0 %all-reduce.5 = (f32[6912]{0:T(1024)S(1)}, f32[768]{0:T(1024)S(1)}, f32[768]{0:T(1024)S(1)}, f32[3072]{0:T(1024)S(1)}, f32[768]{0:T(1024)S(1)}) all-reduce(f32[6912]{0:T(1024)S(1)} %reduce_sum.319, f32[768]{0:T(1024)S(1)} %copy-done.53, f32[768]{0:T(1024)S(1)} %copy-done.62, ...), channel_id=1, replica_groups=mesh['clip'=8,'frame'=4] {'clip','frame'}, use_global_device_ids=true, to_apply=%region_29.30 | all-reduce | flops 12288 | bytes 98304 | tf_op jit(solution)/shard_map/psum | solution.py:288
  1303.3 123.4 %reduce-scatter.10.cloned.1.call-done = f32[432,128]{1,0:T(8,128)} async-done(((f32[13824,128]{1,0:T(8,128)}), f32[432,128]{1,0:T(8,128)}) %reduce-scatter.10.cloned.1.call-update) | async-done | bytes 221200 | tf_op jit(solution)/shard_map/reduce_scatter | solution.py:281
  1428.4 223.6 %reduce-scatter.8.cloned.1.call-done = f32[1296,128]{1,0:T(8,128)} async-done(((f32[41472,128]{1,0:T(8,128)}), f32[1296,128]{1,0:T(8,128)}) %reduce-scatter.8.cloned.1.call-update) | async-done | bytes 663568 | tf_op jit(solution)/shard_map/reduce_scatter | solution.py:280
  (315 shorter events, 399.1 us)
Async XLA Ops:
  7.2 93.8 %all-gather.8.cloned.1.call-start = ((), (), s32[]{:S(2)}) async-start(), calls=%async_computation.11 | async-start | bytes 10948608 | tf_op jit(solution)/shard_map/all_gather | solution.py:128
  8.0 154.4 %all-gather.10.cloned.1.call-start = ((), (), s32[]{:S(2)}) async-start(), calls=%async_computation.12 | async-start | bytes 3649536 | tf_op jit(solution)/shard_map/all_gather | solution.py:130
  8.7 218.6 %all-gather.12.cloned.1.call-start = ((), (), s32[]{:S(2)}) async-start(), calls=%async_computation.13 | async-start | bytes 1216512 | tf_op jit(solution)/shard_map/all_gather | solution.py:131
  9.4 324.0 %all-gather.14.cloned.1.call-start = ((), (), s32[]{:S(2)}) async-start(), calls=%async_computation.14 | async-start | bytes 3649536 | tf_op jit(solution)/shard_map/all_gather | solution.py:133
  13.1 149.3 %copy-start.27 = (f32[2,4,256]{2,1,0:T(4,128)}, f32[2,4,256]{2,1,0:T(4,128)S(1)}, u32[]{:S(2)}) copy-start(f32[2,4,256]{2,1,0:T(4,128)S(1)} %broadcast_multiply_fusion.2) | copy-start | bytes 24580
  16.7 145.7 %copy-start.33 = (f32[2,4,256]{2,1,0:T(4,128)}, f32[2,4,256]{2,1,0:T(4,128)S(1)}, u32[]{:S(2)}) copy-start(f32[2,4,256]{2,1,0:T(4,128)S(1)} %fusion.83) | copy-start | bytes 24580
  61.5 165.9 %copy-start.51 = (f32[768]{0:T(1024)}, f32[768]{0:T(1024)S(1)}, u32[]{:S(2)}) copy-start(f32[768]{0:T(1024)S(1)} %convert_element_type.157) | copy-start | bytes 9220
  61.6 39.4 %copy-start.40 = (f32[2,384]{1,0:T(2,128)}, f32[2,384]{1,0:T(2,128)S(1)}, u32[]{:S(2)}) copy-start(f32[2,384]{1,0:T(2,128)S(1)} %get-tuple-element.60) | copy-start | bytes 9220
  61.6 39.4 %copy-start.42 = (f32[2,384]{1,0:T(2,128)}, f32[2,384]{1,0:T(2,128)S(1)}, u32[]{:S(2)}) copy-start(f32[2,384]{1,0:T(2,128)S(1)} %get-tuple-element.61) | copy-start | bytes 9220
  101.0 61.4 %copy-start.3 = (bf16[2,4,256,768]{3,2,1,0:T(8,128)(2,1)S(1)}, bf16[2,4,256,768]{3,2,1,0:T(8,128)(2,1)}, u32[]{:S(2)}) copy-start(bf16[2,4,256,768]{3,2,1,0:T(8,128)(2,1)} %param.16) | copy-start | bytes 9437188
  107.3 67.5 %copy-start.38 = (f32[2,768]{1,0:T(2,128)}, f32[2,768]{1,0:T(2,128)S(1)}, u32[]{:S(2)}) copy-start(f32[2,768]{1,0:T(2,128)S(1)} %get-tuple-element.58) | copy-start | bytes 18436
  107.3 67.5 %copy-start.55 = (f32[2,768]{1,0:T(2,128)}, f32[2,768]{1,0:T(2,128)S(1)}, u32[]{:S(2)}) copy-start(f32[2,768]{1,0:T(2,128)S(1)} %get-tuple-element.57) | copy-start | bytes 18436
  107.3 120.0 %copy-start.48 = (f32[2,768]{1,0:T(2,128)}, f32[2,768]{1,0:T(2,128)S(1)}, u32[]{:S(2)}) copy-start(f32[2,768]{1,0:T(2,128)S(1)} %get-tuple-element.59) | copy-start | bytes 18436
  107.3 130.3 %copy-start.23 = (f32[2,768]{1,0:T(2,128)}, f32[2,768]{1,0:T(2,128)S(1)}, u32[]{:S(2)}) copy-start(f32[2,768]{1,0:T(2,128)S(1)} %get-tuple-element.55) | copy-start | bytes 18436
  243.5 87.6 %all-to-all-start = ((bf16[2,4,256,768]{3,1,0,2:T(4,128)(2,1)}), bf16[2,4,256,768]{3,1,0,2:T(4,128)(2,1)S(1)}, u32[]{:S(2)}, u32[]{:S(2)}) async-start(bf16[2,4,256,768]{3,1,0,2:T(4,128)(2,1)} %copy.114), calls=%async_computation | async-start | bytes 6291456 | tf_op jit(solution)/shard_map/all_to_all | solution.py:165
  247.2 286.0 %all-gather.16.cloned.1.call-start = ((), (), s32[]{:S(2)}) async-start(), calls=%async_computation.15 | async-start | bytes 1216512 | tf_op jit(solution)/shard_map/all_gather | solution.py:134
  247.8 297.1 %all-gather.18.cloned.1.call-start = ((), (), s32[]{:S(2)}) async-start(), calls=%async_computation.16 | async-start | bytes 4866048 | tf_op jit(solution)/shard_map/all_gather | solution.py:136
  446.5 86.7 %copy-start.37 = (f32[2,768]{1,0:T(2,128)S(1)}, f32[2,768]{1,0:T(2,128)}, u32[]{:S(2)}) copy-start(f32[2,768]{1,0:T(2,128)} %get-tuple-element.56) | copy-start | bytes 18436
  446.5 82.9 %all-to-all-start.1 = ((bf16[2,16,64,768]{3,2,0,1:T(8,128)(2,1)}), bf16[2,16,64,768]{3,2,0,1:T(8,128)(2,1)S(1)}, u32[]{:S(2)}, u32[]{:S(2)}) async-start(bf16[2,16,64,768]{3,2,0,1:T(8,128)(2,1)} %reshape.261), calls=%async_computation.1 | async-start | bytes 6291456 | tf_op jit(solution)/shard_map/all_to_all | solution.py:178
  450.4 119.3 %all-gather.20.cloned.1.call-start = ((), (), s32[]{:S(2)}) async-start(), calls=%async_computation.17 | async-start | bytes 4866048 | tf_op jit(solution)/shard_map/all_gather | solution.py:138
  451.1 798.8 %reduce-scatter.16.cloned.1.call-start = ((), (), s32[]{:S(2)}) async-start(), calls=%async_computation.22 | async-start | bytes 2433024 | tf_op jit(solution)/shard_map/reduce_scatter | solution.py:284
  451.2 90.3 %copy-start.35 = (f32[768]{0:T(1024)}, f32[768]{0:T(1024)S(1)}, u32[]{:S(2)}) copy-start(f32[768]{0:T(1024)S(1)} %convert_element_type.163) | copy-start | bytes 9220
  545.0 59.2 %slice-start.5 = ((s8[6291456]{0:T(1024)(128)(4,1)}), s8[2097152]{0:T(1024)(128)(4,1)S(1)}, s32[]{:S(2)}) async-start(s8[6291456]{0:T(1024)(128)(4,1)} %bitcast.258), calls=%async_computation.30 | async-start | bytes 4194304
  652.3 641.3 %reduce-scatter.18.cloned.1.call-start = ((), (), s32[]{:S(2)}) async-start(), calls=%async_computation.23 | async-start | bytes 9732096 | tf_op jit(solution)/shard_map/reduce_scatter | solution.py:285
  691.5 85.7 %all-to-all-start.2 = ((bf16[2,4,256,768]{3,1,0,2:T(4,128)(2,1)}), bf16[2,4,256,768]{3,1,0,2:T(4,128)(2,1)}, u32[]{:S(2)}, u32[]{:S(2)}) async-start(bf16[2,4,256,768]{3,1,0,2:T(4,128)(2,1)} %copy.122), calls=%async_computation.2 | async-start | bytes 6291456 | tf_op jit(solution)/shard_map/all_to_all | solution.py:216
  696.2 599.2 %reduce-scatter.20.cloned.1.call-start = ((), (), s32[]{:S(2)}) async-start(), calls=%async_computation.24 | async-start | bytes 9732096 | tf_op jit(solution)/shard_map/reduce_scatter | solution.py:286
  696.4 112.1 %copy-start.7 = (f32[2,64,12,16]{3,2,1,0:T(8,128)}, f32[2,64,12,16]{3,2,1,0:T(8,128)S(1)}, u32[]{:S(2)}) copy-start(f32[2,64,12,16]{3,2,1,0:T(8,128)S(1)} %log_add_fusion) | copy-start | bytes 294916
  724.3 572.8 %reduce-scatter.12.cloned.1.call-start = ((), (), s32[]{:S(2)}) async-start(), calls=%async_computation.20 | async-start | bytes 2433024 | tf_op jit(solution)/shard_map/reduce_scatter | solution.py:282
  918.7 94.2 %slice-start.3 = ((s8[6291456]{0:T(1024)(128)(4,1)}), s8[4194304]{0:T(1024)(128)(4,1)S(1)}, s32[]{:S(2)}) async-start(s8[6291456]{0:T(1024)(128)(4,1)} %bitcast.246), calls=%async_computation.28 | async-start | bytes 8388608
  1041.6 260.1 %reduce-scatter.14.cloned.1.call-start = ((), (), s32[]{:S(2)}) async-start(), calls=%async_computation.21 | async-start | bytes 7299072 | tf_op jit(solution)/shard_map/reduce_scatter | solution.py:283
  1062.5 364.3 %reduce-scatter.10.cloned.1.call-start = ((), (), s32[]{:S(2)}) async-start(), calls=%async_computation.19 | async-start | bytes 7299072 | tf_op jit(solution)/shard_map/reduce_scatter | solution.py:281
  1190.6 461.5 %reduce-scatter.8.cloned.1.call-start = ((), (), s32[]{:S(2)}) async-start(), calls=%async_computation.18 | async-start | bytes 21897216 | tf_op jit(solution)/shard_map/reduce_scatter | solution.py:280
  (66 other events, 517.3 us)
Sparse Core Ops, SparseCore 0:
  10.9 90.0 all-gather.7
  103.8 58.5 all-gather.9
  165.2 52.8 all-gather.11
  220.8 95.2 all-gather.13
  318.7 56.9 all-gather.15
  378.3 62.4 all-gather.17
  454.0 99.0 all-gather.19
  652.4 131.3 reduce-scatter.15
  790.8 133.6 reduce-scatter.17
  930.2 143.9 reduce-scatter.19
  1080.3 98.0 reduce-scatter.11
  1183.9 117.7 reduce-scatter.13
  1308.3 118.4 reduce-scatter.9
  1433.1 218.9 reduce-scatter.7
where the time goes:
time: 1670 us; the launch traced here: 1660 us
  waiting for transfers between devices  663 us (40%)
  matrix products  410 us (25%)
  local copies, waits for them, and re-layouts  266 us (16%)
  blocking collectives  176 us (11%)
  other arithmetic  117 us (7%)
    reduce_scatter x1, waiting for transfers between devices, shards(): lax.psum_scatter(as_lanes(grad_ada), ('clip', 'frame'), scatter_dimension...  224 us
    reduce_scatter x1, waiting for transfers between devices, shards(): lax.psum_scatter(as_lanes(grad_sqkv), ('clip', 'frame'), scatter_dimensio...  123 us
    all_to_all x1, blocking collectives, shards(): lax.all_to_all(grad_patch_hidden, 'frame', split_axis=1, concat_axis=2, t...  93.3 us
    dot_general x6, matrix products, project(): jnp.einsum('cfpd,dk->cfpk', left, right, preferred_element_type=jnp.float32)  88 us
    dot_general x6, matrix products, project_back(): jnp.einsum('cfpk,dk->cfpd', left, right, preferred_element_type=jnp.float32)  82.8 us
    all_to_all x1, waiting for transfers between devices, shards(): lax.all_to_all(hidden_two, 'frame', split_axis=2, concat_axis=1, tiled=True)  82.7 us
    all_to_all x1, waiting for transfers between devices, shards(): lax.all_to_all(patch_mixed, 'frame', split_axis=1, concat_axis=2, tiled=T...  78.2 us
    dot_general x6, matrix products, weight_term(): jnp.einsum('cfpd,cfpk->dk', left, right, preferred_element_type=jnp.float32)  74.9 us
  transfers between devices with their start and end apart: 17, of which 8 were waited for; matrix products, arithmetic and copies ran while one was open for 42% of the time, Pallas kernels for 0%

commit v1 on v0

v1 whole, which is shorter than its diff:
```python
import functools
import math

import jax
import jax.numpy as jnp
from jax import lax
from jax.experimental import pallas as pl
from jax.experimental.pallas import tpu as pltpu
from jax.sharding import PartitionSpec as P

HEADS = 12
HEAD = 64
PAIRS = HEADS // 2
ROWS = 32
GELU_C = math.sqrt(2.0 / math.pi)
GELU_A = 0.044715
VMEM_LIMIT = 58 << 20

f32 = jnp.float32
bf16 = jnp.bfloat16
highest = lax.Precision.HIGHEST
MESH = pl.DeviceIdType.MESH
VMEM = pltpu.VMEM
DMA = pltpu.SemaphoreType.DMA


def embed_steps(time_steps, model_width):
    half_width = model_width // 2
    frequencies = jnp.exp(
        -math.log(10000.0) * jnp.arange(half_width, dtype=f32) / half_width
    )
    angles = time_steps.astype(f32)[:, None] * frequencies[None, :]
    return jnp.concatenate([jnp.cos(angles), jnp.sin(angles)], axis=1)


def dot(left, right, left_dim, right_dim):
    return lax.dot_general(
        left, right, (((left_dim,), (right_dim,)), ((), ())), preferred_element_type=f32
    )


def flip(index, mask):
    bit = 1
    while bit <= mask:
        if mask & bit:
            index = index + bit * (1 - 2 * ((index // bit) % 2))
        bit *= 2
    return index


def span(masks):
    out = [0]
    for mask in masks:
        out = out + [entry ^ mask for entry in out]
    return out


def frame_masks(frames):
    masks, bit = [], 1
    while bit < frames:
        masks.append(bit)
        bit *= 2
    if len(masks) > 1:
        masks = [frames - 1] + masks[:-1]
    return masks


def clip_tail_masks(clips):
    masks, bit = [], 2
    while bit < clips:
        masks.append(bit)
        bit *= 2
    return masks


def greet(clips, frames):
    clip, frame = lax.axis_index("clip"), lax.axis_index("frame")
    barrier = pltpu.get_barrier_semaphore()
    for step in range(1, clips):
        pl.semaphore_signal(
            barrier, inc=1, device_id={"clip": lax.rem(clip + step, clips)}, device_id_type=MESH
        )
    for step in range(1, frames):
        pl.semaphore_signal(
            barrier, inc=1, device_id={"frame": lax.rem(frame + step, frames)}, device_id_type=MESH
        )
    pl.semaphore_wait(barrier, clips + frames - 2)


def spread(axis, size, source_of, target, send_sems, recv_sems):
    me = lax.axis_index(axis)
    copies = []
    for step in range(1, size):
        peer = lax.rem(me + step, size)
        copy = pltpu.make_async_remote_copy(
            src_ref=source_of(peer),
            dst_ref=target.at[me],
            send_sem=send_sems.at[step - 1],
            recv_sem=recv_sems.at[step - 1],
            device_id={axis: peer},
            device_id_type=MESH,
        )
        copy.start()
        copies.append(copy)
    return copies


def start_kernel(
    clips, frames, clip_count,
    x_ref, cotangent, sh_c, sh_b, sh_u, sh_d, embed, select, ada, bias,
    w_c, w_b, w_u, w_d, mod, chosen, totals, hidden_out, qkv_out, mixed_out, branch_out,
    after_first, after_later, cot_first,
    v_c, z_c, z_b, z_u, z_d, st_w, b_c, b_b, b_u, b_d,
    embeds, parts, terms, arrived, held, lined, hidden, qkv, mixed, branch, after,
    zs, zr, cs, cr, xs, xr, ls, es, er, ps, pr, fs, fr, ts, tr, hs, hr, os, ws,
):
    clip, frame = lax.axis_index("clip"), lax.axis_index("frame")
    shards_in = (sh_c, sh_b, sh_u, sh_d)
    zoned = (z_c, z_b, z_u, z_d)
    blocks = (b_c, b_b, b_u, b_d)
    wholes = (v_c, w_b, w_u, w_d)
    width = mod.shape[1]
    frame_count, tokens = x_ref.shape[1], x_ref.shape[2]
    part = tokens // frames
    greet(clips, frames)
    masks = frame_masks(frames)
    sends = []
    stage = {}

    def frame_step(group, step):
        number = (1 << step) - 1
        copies = []
        for offset in span(masks[:step]):
            slot = flip(frame, offset)
            source = shards_in[group] if offset == 0 else zoned[group].at[slot]
            copy = pltpu.make_async_remote_copy(
                src_ref=source,
                dst_ref=zoned[group].at[slot],
                send_sem=zs.at[group, number],
                recv_sem=zr.at[group, number],
                device_id={"frame": flip(frame, masks[step])},
                device_id_type=MESH,
            )
            copy.start()
            copies.append(copy)
            number += 1
        sends.extend(copies)
        stage[group] = copies

    def frame_rest(group):
        for step in range(1, len(masks)):
            for copy in stage[group]:
                copy.wait_recv()
            frame_step(group, step)

    tail = clip_tail_masks(clips)
    steps = len(tail)
    orders = (tail, tail[::-1])
    moving = {}

    def block_send(group, half, step, position, offset):
        whole = wholes[group]
        block_rows = whole.shape[0] // clips
        columns = whole.shape[1] // 2
        rows = pl.ds(pl.multiple_of(flip(clip, offset) * block_rows, block_rows), block_rows)
        lanes = pl.ds(half * columns, columns)
        target = whole.at[rows, lanes]
        number = (1 << step) - 1 + position
        copy = pltpu.make_async_remote_copy(
            src_ref=blocks[group].at[:, lanes] if offset == 0 else target,
            dst_ref=target,
            send_sem=xs.at[group, half, number],
            recv_sem=xr.at[group, half, number],
            device_id={"clip": flip(clip, orders[half][step])},
            device_id_type=MESH,
        )
        copy.start()
        moving[group, half, number] = copy

    core_copies = {group: [] for group in range(4)}

    def core_send(group, offset):
        whole = wholes[group]
        block_rows = whole.shape[0] // clips
        rows = pl.ds(pl.multiple_of(flip(clip, offset) * block_rows, block_rows), block_rows)
        number = len(core_copies[group])
        copy = pltpu.make_async_remote_copy(
            src_ref=blocks[group] if offset == 0 else whole.at[rows, :],
            dst_ref=whole.at[rows, :],
            send_sem=cs.at[group, number],
            recv_sem=cr.at[group, number],
            device_id={"clip": flip(clip, 1)},
            device_id_type=MESH,
        )
        copy.start()
        core_copies[group].append(copy)

    local_copies = []

    def block_ready(group):
        for copy in stage[group]:
            copy.wait_recv()
        rows, columns = shards_in[group].shape
        block_rows = frames * rows
        if rows % 16:
            for slot in range(frames):
                st_w[slot * rows : (slot + 1) * rows, :columns] = zoned[group][slot].astype(f32)
            blocks[group][...] = st_w[:block_rows, :columns].astype(bf16)
        else:
            for slot in range(frames):
                blocks[group][slot * rows : (slot + 1) * rows, :] = zoned[group][slot]
        for step in range(steps):
            for half in range(2):
                block_send(group, half, step, 0, 0)
        core_send(group, 0)
        place = pl.ds(pl.multiple_of(clip * block_rows, block_rows), block_rows)
        keep = pltpu.make_async_copy(blocks[group], wholes[group].at[place, :], ls.at[group])
        keep.start()
        local_copies.append(keep)

    def block_forward(group):
        for step in range(1, steps):
            for half in range(2):
                for position in range(1 << (step - 1), 1 << step):
                    moving[group, half, position - 1].wait_recv()
                for later in range(step, steps):
                    for position, offset in enumerate(span(orders[half][:later])):
                        if (1 << (step - 1)) <= position < (1 << step):
                            block_send(group, half, later, position, offset)

    def block_finish(group):
        last = (1 << (steps - 1)) - 1
        for half in range(2):
            for number in range(last, (1 << steps) - 1):
                moving[group, half, number].wait_recv()
        for offset in span(tail)[1:]:
            core_send(group, offset)

    def core_finish(group):
        for copy in core_copies[group]:
            copy.wait_recv()

    for group in range(4):
        frame_step(group, 0)
    own = spread("clip", clips, lambda peer: embed, embeds, es, er)
    sends.extend(own)
    embeds[clip] = embed[...]
    for group in range(4):
        zoned[group][frame] = shards_in[group][...]
    for copy in own:
        copy.wait_recv()
    picked = dot(embeds[...].reshape(clips * 16, width), select[...], 1, 0).astype(bf16)
    chosen[...] = picked
    parts[...] = dot(picked, ada[...], 1, 0)
    for peer in range(clips):
        for local in range(clip_count):
            row = peer * 16 + local
            for piece in range(9):
                terms[peer, local * 9 + piece : local * 9 + piece + 1, :] = (
                    parts[row : row + 1, piece * width : (piece + 1) * width]
                    + bias[piece : piece + 1, :]
                )
        base = clip_count * 9
        terms[peer, base : base + 7, :] = bias[9:16, :]
        if base + 7 < ROWS:
            terms[peer, base + 7 : ROWS, :] = jnp.zeros((ROWS - base - 7, width), f32)
    own = spread("clip", clips, lambda peer: terms.at[peer], arrived, ps, pr)
    sends.extend(own)
    arrived[clip] = terms[clip]
    frame_rest(0)
    for copy in own:
        copy.wait_recv()
    total = arrived[0]
    for peer in range(1, clips):
        total = total + arrived[peer]
    held[...] = total
    own = spread("frame", frames, lambda peer: held, lined, fs, fr)
    sends.extend(own)
    lined[frame] = total
    block_ready(0)
    for group in range(1, 4):
        frame_rest(group)

    cot_copies = []
    for step in range(1, frames):
        peer = lax.rem(frame + step, frames)
        copy = pltpu.make_async_remote_copy(
            src_ref=cotangent.at[0, :, pl.ds(pl.multiple_of(peer * part, part), part), :],
            dst_ref=cot_first.at[frame],
            send_sem=ts.at[step - 1],
            recv_sem=tr.at[step - 1],
            device_id={"frame": peer},
            device_id_type=MESH,
        )
        copy.start()
        cot_copies.append(copy)
    keep = pltpu.make_async_copy(
        cotangent.at[0, :, pl.ds(pl.multiple_of(frame * part, part), part), :],
        cot_first.at[frame],
        ls.at[4],
    )
    keep.start()
    local_copies.append(keep)

    for copy in own:
        copy.wait_recv()
    total = lined[0]
    for peer in range(1, frames):
        total = total + lined[peer]
    mod[...] = total
    block_forward(0)
    for group in range(1, 4):
        block_ready(group)
    block_finish(0)
    core_finish(0)
    local_copies[0].wait()

    keep = pltpu.make_async_copy(v_c, w_c, ls.at[5])
    keep.start()
    local_copies.append(keep)

    def after_copy(f, step):
        peer = lax.rem(frame + step, frames)
        return pltpu.make_async_remote_copy(
            src_ref=after.at[f, pl.ds(pl.multiple_of(peer * part, part), part), :],
            dst_ref=after_first.at[frame, f],
            send_sem=hs.at[f, step - 1],
            recv_sem=hr.at[f, step - 1],
            device_id={"frame": peer},
            device_id_type=MESH,
        )

    def own_after(f):
        return pltpu.make_async_copy(
            after.at[f, pl.ds(pl.multiple_of(frame * part, part), part), :],
            after_first.at[frame, f],
            os.at[f],
        )

    def later_after(f):
        return pltpu.make_async_copy(after.at[f], after_later.at[f - frame_count], os.at[f])

    kept = ((hidden, hidden_out), (qkv, qkv_out), (mixed, mixed_out), (branch, branch_out))

    def write_back(f):
        return [
            pltpu.make_async_copy(source.at[f], target.at[f], ws.at[number, f])
            for number, (source, target) in enumerate(kept)
        ]

    for local in range(clip_count):
        row = local * 9

        def one_frame(index, carry):
            f = local * frame_count + index
            values = x_ref[local, index].astype(f32)
            norm, _ = normed(values)
            scaled = norm * (1.0 + mod[row + 1 : row + 2, :]) + mod[row : row + 1, :]
            lowered = scaled.astype(bf16)
            hidden[f] = lowered
            qkv[f] = dot(lowered, v_c[:, : 3 * width], 1, 0).astype(bf16)
            attend(qkv.at[f], mixed.at[f], totals.at[f], width, None)
            grown = dot(mixed[f], v_c[:, 3 * width :], 1, 0) + mod[18:19, :]
            branch[f] = grown.astype(bf16)
            after[f] = (values + mod[row + 2 : row + 3, :] * grown).astype(bf16)
            if local == 0:
                for step in range(1, frames):
                    after_copy(f, step).start()
                own_after(f).start()
            else:
                later_after(f).start()
            for copy in write_back(f):
                copy.start()
            return carry

        lax.fori_loop(0, frame_count, one_frame, 0)
        if local == 0:
            block_forward(1)
    for group in range(2, 4):
        block_forward(group)
    for group in range(1, 4):
        block_finish(group)
    for group in range(1, 4):
        core_finish(group)

    def settle(f, carry):
        for step in range(1, frames):
            copy = after_copy(f, step)
            copy.wait_recv()
            copy.wait_send()
        own_after(f).wait()
        return carry

    lax.fori_loop(0, frame_count, settle, 0)

    def settle_later(f, carry):
        later_after(f).wait()
        return carry

    lax.fori_loop(frame_count, clip_count * frame_count, settle_later, 0)

    def settle_kept(f, carry):
        for copy in write_back(f):
            copy.wait()
        return carry

    lax.fori_loop(0, clip_count * frame_count, settle_kept, 0)
    for copy in cot_copies:
        copy.wait_recv()
        copy.wait_send()
    for copy in local_copies[1:]:
        copy.wait()
    for copy in moving.values():
        copy.wait_send()
    for group in range(4):
        for copy in core_copies[group]:
            copy.wait_send()
    for copy in sends:
        copy.wait_send()


def start_call(
    clips, frames, inputs, cotangent, sh_c, sh_b, sh_u, sh_d, embed, select, ada, bias
):
    clip_count, frame_count, tokens, width = inputs.shape
    rows, columns = sh_c.shape
    rows_d = sh_d.shape[0]
    block = frames * rows
    block_d = frames * rows_d
    peers = max(clips // 2 - 1, 1)
    total = clip_count * frame_count
    part = tokens // frames
    whole = jax.ShapeDtypeStruct((clips * block, columns), bf16)
    vmem = pl.BlockSpec(memory_space=VMEM)
    hbm = pl.BlockSpec(memory_space=pl.ANY)
    zoned = lambda height, lanes: VMEM((frames, height, lanes), bf16)
    saved = lambda lanes: jax.ShapeDtypeStruct((total, tokens, lanes), bf16)
    lent = lambda lanes: VMEM((total, tokens, lanes), bf16)
    traded = jax.ShapeDtypeStruct((frames, frame_count, part, width), bf16)
    return pl.pallas_call(
        functools.partial(start_kernel, clips, frames, clip_count),
        out_shape=(
            whole, whole, whole,
            jax.ShapeDtypeStruct((clips * block_d, width), bf16),
            jax.ShapeDtypeStruct((ROWS, width), f32),
            jax.ShapeDtypeStruct((clips * 16, 128), bf16),
            jax.ShapeDtypeStruct((total, 16, tokens), f32),
            saved(width), saved(3 * width), saved(width), saved(width),
            traded,
            jax.ShapeDtypeStruct(((clip_count - 1) * frame_count, tokens, width), bf16),
            traded,
        ),
        in_specs=[vmem, hbm] + [vmem] * 8,
        out_specs=(hbm, hbm, hbm, hbm, vmem, vmem, vmem) + (hbm,) * 7,
        scratch_shapes=[
            VMEM((clips * block, columns), bf16),
            zoned(rows, columns), zoned(rows, columns), zoned(rows, columns), zoned(rows_d, width),
            VMEM((max(block, block_d), columns), f32),
            VMEM((block, columns), bf16),
            VMEM((block, columns), bf16),
            VMEM((block, columns), bf16),
            VMEM((block_d, width), bf16),
            VMEM((clips, 16, width), bf16),
            VMEM((clips * 16, 9 * width), f32),
            VMEM((clips, ROWS, width), f32),
            VMEM((clips, ROWS, width), f32),
            VMEM((ROWS, width), f32),
            VMEM((frames, ROWS, width), f32),
            lent(width), lent(3 * width), lent(width), lent(width), lent(width),
            DMA((4, frames - 1)), DMA((4, frames - 1)),
            DMA((4, clips // 2)), DMA((4, clips // 2)),
            DMA((4, 2, peers)), DMA((4, 2, peers)),
            DMA((6,)),
            DMA((clips - 1,)), DMA((clips - 1,)),
            DMA((clips - 1,)), DMA((clips - 1,)),
            DMA((frames - 1,)), DMA((frames - 1,)),
            DMA((frames - 1,)), DMA((frames - 1,)),
            DMA((frame_count, frames - 1)), DMA((frame_count, frames - 1)),
            DMA((total,)),
            DMA((4, total)),
        ],
        compiler_params=pltpu.CompilerParams(
            collective_id=0, has_side_effects=True, vmem_limit_bytes=VMEM_LIMIT
        ),
    )(inputs, cotangent, sh_c, sh_b, sh_u, sh_d, embed, select, ada, bias)


def end_kernel(clips, frames, small, out, lined, held, fs, fr, ps, pr):
    clip, frame = lax.axis_index("clip"), lax.axis_index("frame")
    greet(clips, frames)
    first = spread("frame", frames, lambda peer: small, lined, fs, fr)
    lined[frame] = small[...]
    for copy in first:
        copy.wait_recv()
    total = lined[0]
    for peer in range(1, frames):
        total = total + lined[peer]
    held[...] = total
    second = spread("clip", clips, lambda peer: held, out, ps, pr)
    out[clip] = total
    for copy in second:
        copy.wait_recv()
    for copy in first + second:
        copy.wait_send()


def end_call(clips, frames, small):
    vmem = pl.BlockSpec(memory_space=VMEM)
    return pl.pallas_call(
        functools.partial(end_kernel, clips, frames),
        out_shape=jax.ShapeDtypeStruct((clips,) + small.shape, f32),
        in_specs=[vmem],
        out_specs=vmem,
        scratch_shapes=[
            VMEM((frames,) + small.shape, f32),
            VMEM(small.shape, f32),
            DMA((frames - 1,)), DMA((frames - 1,)),
            DMA((clips - 1,)), DMA((clips - 1,)),
        ],
        compiler_params=pltpu.CompilerParams(collective_id=1, has_side_effects=True),
    )(small)


def normed(values):
    centred = values - jnp.mean(values, axis=-1, keepdims=True)
    scale = lax.rsqrt(jnp.mean(centred * centred, axis=-1, keepdims=True) + 1e-06)
    return centred * scale, scale


def norm_back(grad, scaled, norm, scale):
    inner = grad * scaled
    return scale * (
        inner
        - jnp.mean(inner, axis=-1, keepdims=True)
        - norm * jnp.mean(inner * norm, axis=-1, keepdims=True)
    )


def column_sum(values):
    return jnp.sum(values, axis=0, keepdims=True)


def attend(qkv, mixed, totals, width, mask):
    tokens = qkv.shape[0]
    low = lax.broadcasted_iota(jnp.int32, (tokens, 128), 1) < HEAD
    for pair in range(PAIRS):
        at = pair * 128
        queries = qkv[:, at : at + 128] * bf16(0.125)
        keys = qkv[:, width + at : width + at + 128]
        values = qkv[:, 2 * width + at : 2 * width + at + 128]
        halves = []
        for half in range(2):
            own = jnp.where(low if half == 0 else ~low, queries, bf16(0))
            scores = dot(keys, own, 1, 1)
            if mask is not None:
                scores = scores + mask[...]
            peak = jnp.max(scores, axis=0, keepdims=True)
            terms = jnp.exp(scores - peak)
            total = jnp.sum(terms, axis=0, keepdims=True)
            weights = (terms * (1.0 / total)).astype(bf16)
            totals[2 * pair + half : 2 * pair + half + 1, :] = peak + jnp.log(total)
            halves.append(dot(weights, values, 0, 0))
        mixed[:, at : at + 128] = jnp.where(low, halves[0], halves[1]).astype(bf16)


def attend_back(qkv, grad_mixed, totals, grad_qkv, width, mask):
    tokens = qkv.shape[0]
    low = lax.broadcasted_iota(jnp.int32, (tokens, 128), 1) < HEAD
    for pair in range(PAIRS):
        at = pair * 128
        queries = qkv[:, at : at + 128]
        keys = qkv[:, width + at : width + at + 128]
        values = qkv[:, 2 * width + at : 2 * width + at + 128]
        grads = grad_mixed[:, at : at + 128]
        halves = []
        for half in range(2):
            pick = low if half == 0 else ~low
            own = jnp.where(pick, queries * bf16(0.125), bf16(0))
            own_grads = jnp.where(pick, grads, bf16(0))
            scores = dot(keys, own, 1, 1)
            if mask is not None:
                scores = scores + mask[...]
            weights = jnp.exp(scores - totals[2 * pair + half : 2 * pair + half + 1, :])
            grad_weights = dot(values, own_grads, 1, 1)
            inner = jnp.sum(weights * grad_weights, axis=0, keepdims=True)
            grad_scores = (weights * (grad_weights - inner)).astype(bf16)
            halves.append(
                (
                    dot(grad_scores, keys, 0, 0),
                    dot(grad_scores, queries, 1, 0),
                    dot(weights.astype(bf16), grads, 1, 0),
                )
            )
        for part, factor in ((0, 0.125), (1, 0.125), (2, 1.0)):
            joined = jnp.where(low, halves[0][part], halves[1][part]) * factor
            start = part * width + at
            grad_qkv[:, start : start + 128] = joined.astype(bf16)


def full(shape):
    return pl.BlockSpec(shape, lambda *_: (0,) * len(shape), pipeline_mode=pl.Buffered(1))


def middle_kernel(
    clip, after_ref, cot_ref, loss, mod, w_b, w_u, w_d,
    out_ref, grad_ref, act_ref, gup_ref, h3_ref, gb3_ref, mixed_ref, gb2_ref, h2_ref, gqkv_ref, sums,
    qkv, totals, mask, gmix,
):
    width = after_ref.shape[-1]
    group = after_ref.shape[2]
    tokens = after_ref.shape[0] * after_ref.shape[1] * group
    row = clip * 9
    piece = lambda number: mod[row + number : row + number + 1, :]

    @pl.when(pl.program_id(0) == 0)
    def _():
        sums[...] = jnp.zeros_like(sums)
        first = lax.broadcasted_iota(jnp.int32, (tokens, tokens), 0)
        second = lax.broadcasted_iota(jnp.int32, (tokens, tokens), 1)
        mask[...] = jnp.where(lax.rem(first, group) == lax.rem(second, group), 0.0, -1e30)

    def add(place, values):
        sums[place : place + 1, :] += values

    after = after_ref[...].reshape(tokens, width).astype(f32)
    norm, scale = normed(after)
    hidden = (norm * (1.0 + piece(4)) + piece(3)).astype(bf16)
    h2_ref[...] = hidden
    qkv[...] = dot(hidden, w_b[:, : 3 * width], 1, 0).astype(bf16)
    attend(qkv, mixed_ref, totals, width, mask)
    branch_two = dot(mixed_ref[...], w_b[:, 3 * width :], 1, 0) + mod[19:20, :]
    after_two = after + piece(5) * branch_two
    norm_three, scale_three = normed(after_two)
    hidden = (norm_three * (1.0 + piece(7)) + piece(6)).astype(bf16)
    h3_ref[...] = hidden
    grad_out = cot_ref[...].reshape(tokens, width).astype(f32) * loss[clip : clip + 1, :]
    grad_branch = (grad_out * piece(8)).astype(bf16)
    gb3_ref[...] = grad_branch
    add(11, column_sum(grad_branch.astype(f32)))
    branch_three = jnp.zeros((tokens, width), f32)
    grad_hidden = jnp.zeros((tokens, width), f32)
    for chunk in range(w_u.shape[1] // width):
        part = slice(chunk * width, (chunk + 1) * width)
        upper = dot(hidden, w_u[:, part], 1, 0) + mod[20 + chunk : 21 + chunk, :]
        square = upper * upper
        bend = jnp.tanh(upper * (GELU_C + (GELU_C * GELU_A) * square))
        half = 0.5 + 0.5 * bend
        act = (upper * half).astype(bf16)
        slope = half + (0.5 * upper) * (1.0 - bend * bend) * (
            GELU_C + (3.0 * GELU_C * GELU_A) * square
        )
        act_ref[:, part] = act
        branch_three += dot(act, w_d[part, :], 1, 0)
        grad_upper = (dot(grad_branch, w_d[part, :], 1, 1) * slope).astype(bf16)
        gup_ref[:, part] = grad_upper
        add(7 + chunk, column_sum(grad_upper.astype(f32)))
        grad_hidden += dot(grad_upper, w_u[:, part], 1, 1)
    branch_three += mod[24:25, :]
    out = (after_two + piece(8) * branch_three).astype(bf16)
    out_ref[...] = out.reshape(out_ref.shape)
    add(5, column_sum(grad_out * branch_three))
    add(3, column_sum(grad_hidden))
    add(4, column_sum(grad_hidden * norm_three))
    grad_two = grad_out + norm_back(grad_hidden, 1.0 + piece(7), norm_three, scale_three)
    add(2, column_sum(grad_two * branch_two))
    grad_branch = (grad_two * piece(5)).astype(bf16)
    gb2_ref[...] = grad_branch
    add(6, column_sum(grad_branch.astype(f32)))
    gmix[...] = dot(grad_branch, w_b[:, 3 * width :], 1, 1).astype(bf16)
    attend_back(qkv, gmix, totals, gqkv_ref, width, mask)
    grad_hidden = dot(gqkv_ref[...], w_b[:, : 3 * width], 1, 1).astype(bf16).astype(f32)
    add(0, column_sum(grad_hidden))
    add(1, column_sum(grad_hidden * norm))
    grad_one = grad_two + norm_back(grad_hidden, 1.0 + piece(4), norm, scale)
    grad_ref[...] = grad_one.astype(bf16).reshape(grad_ref.shape)


def middle_kernel_next(count, clip, *refs):
    middle_kernel(clip, *refs[:7], *refs[7 + count :])


def middle_call(clip, clip_count, after, cot, loss, mod, w_b, w_u, w_d, earlier):
    frames, frame_count, part, width = after.shape
    group = min(16, part)
    tiles = part // group
    tokens = frames * frame_count * group
    hidden_width = w_u.shape[1]
    block = pl.BlockSpec((frames, frame_count, group, width), lambda t: (0, 0, t, 0))
    widths = (hidden_width, hidden_width, width, width, width, width, width, 3 * width)
    own = lambda columns: pl.BlockSpec((tokens, columns), lambda t: (clip * tiles + t, 0))
    rows = tiles * tokens
    in_specs = [
        block, block, full(loss.shape), full(mod.shape), full(w_b.shape), full(w_u.shape),
        full(w_d.shape),
    ]
    args = [after, cot, loss, mod, w_b, w_u, w_d]
    body = functools.partial(middle_kernel, clip)
    aliases = {}
    if earlier is not None:
        in_specs += [pl.BlockSpec(memory_space=pl.ANY)] * len(earlier)
        args += list(earlier)
        aliases = {7 + number: 2 + number for number in range(len(earlier))}
        body = functools.partial(middle_kernel_next, len(earlier), clip)
    return pl.pallas_call(
        body,
        grid=(tiles,),
        in_specs=in_specs,
        out_specs=[block, block] + [own(columns) for columns in widths]
        + [pl.BlockSpec((16, width), lambda t: (0, 0))],
        out_shape=[
            jax.ShapeDtypeStruct(after.shape, bf16), jax.ShapeDtypeStruct(after.shape, bf16),
        ]
        + [jax.ShapeDtypeStruct((clip_count * rows, columns), bf16) for columns in widths]
        + [jax.ShapeDtypeStruct((16, width), f32)],
        scratch_shapes=[
            VMEM((tokens, 3 * width), bf16),
            VMEM((16, tokens), f32),
            VMEM((tokens, tokens), f32),
            VMEM((tokens, width), bf16),
        ],
        input_output_aliases=aliases,
        compiler_params=pltpu.CompilerParams(vmem_limit_bytes=VMEM_LIMIT),
        cost_estimate=pl.CostEstimate(
            flops=rows * 100_000_000, bytes_accessed=rows * 40_000, transcendentals=0
        ),
    )(*args)


def space_back_kernel(
    clip, grad_ref, x_ref, mod, w_c, qkv, branch, totals,
    out_ref, gb_ref, gqkv_ref, sums, gmix,
):
    width = x_ref.shape[-1]
    tokens = x_ref.shape[-2]
    row = clip * 9
    piece = lambda number: mod[row + number : row + number + 1, :]

    @pl.when(pl.program_id(0) == 0)
    def _():
        sums[...] = jnp.zeros_like(sums)

    grad = grad_ref[...].reshape(tokens, width).astype(f32)
    grad_branch = (grad * piece(2)).astype(bf16)
    gb_ref[...] = grad_branch
    sums[2:3, :] += column_sum(grad * branch[...].astype(f32))
    sums[3:4, :] += column_sum(grad_branch.astype(f32))
    gmix[...] = dot(grad_branch, w_c[:, 3 * width :], 1, 1).astype(bf16)
    attend_back(qkv, gmix, totals, gqkv_ref, width, None)
    grad_hidden = dot(gqkv_ref[...], w_c[:, : 3 * width], 1, 1)
    norm, scale = normed(x_ref[...].reshape(tokens, width).astype(f32))
    sums[0:1, :] += column_sum(grad_hidden)
    sums[1:2, :] += column_sum(grad_hidden * norm)
    result = grad + norm_back(grad_hidden, 1.0 + piece(1), norm, scale)
    out_ref[...] = result.reshape(out_ref.shape)


def space_back_next(count, clip, *refs):
    space_back_kernel(clip, *refs[:7], *refs[7 + count :])


def space_back_call(clip, grad, x, mod, w_c, qkv, branch, totals, earlier):
    clip_count, frame_count, tokens, width = x.shape
    frames = grad.shape[0]
    part = grad.shape[2]
    rows = frame_count * tokens
    by_frame = lambda columns: pl.BlockSpec(
        (None, tokens, columns), lambda f: (clip * frame_count + f, 0, 0)
    )
    own = lambda columns: pl.BlockSpec((tokens, columns), lambda f: (clip * frame_count + f, 0))
    in_specs = [
        pl.BlockSpec((frames, 1, part, width), lambda f: (0, f, 0, 0)),
        pl.BlockSpec((1, 1, tokens, width), lambda f: (clip, f, 0, 0)),
        full(mod.shape),
        full(w_c.shape),
        by_frame(3 * width),
        by_frame(width),
        pl.BlockSpec((None, 16, tokens), lambda f: (clip * frame_count + f, 0, 0)),
    ]
    args = [grad, x, mod, w_c, qkv, branch, totals]
    body = functools.partial(space_back_kernel, clip)
    aliases = {}
    if earlier is not None:
        in_specs += [pl.BlockSpec(memory_space=pl.ANY)] * len(earlier)
        args += list(earlier)
        aliases = {7 + number: number for number in range(len(earlier))}
        body = functools.partial(space_back_next, len(earlier), clip)
    return pl.pallas_call(
        body,
        grid=(frame_count,),
        in_specs=in_specs,
        out_specs=[
            pl.BlockSpec((1, 1, tokens, width), lambda f: (clip, f, 0, 0)),
            own(width),
            own(3 * width),
            pl.BlockSpec((8, width), lambda f: (0, 0)),
        ],
        out_shape=[
            jax.ShapeDtypeStruct(x.shape, f32),
            jax.ShapeDtypeStruct((clip_count * rows, width), bf16),
            jax.ShapeDtypeStruct((clip_count * rows, 3 * width), bf16),
            jax.ShapeDtypeStruct((8, width), f32),
        ],
        scratch_shapes=[VMEM((tokens, width), bf16)],
        input_output_aliases=aliases,
        compiler_params=pltpu.CompilerParams(vmem_limit_bytes=VMEM_LIMIT),
        cost_estimate=pl.CostEstimate(
            flops=rows * 20_000_000, bytes_accessed=rows * width * 20, transcendentals=0
        ),
    )(*args)


def scatter_rows(grad):
    return lax.psum_scatter(
        grad, ("clip", "frame"), scatter_dimension=0, tiled=True
    ).astype(f32)


def shards(
    inputs, cotangent, time_steps, weight_index, ada_weight, ada_bias, space_qkv, space_out,
    space_out_bias, time_qkv, time_out, time_out_bias, up_weight, up_bias, down_weight, down_bias,
):
    clip_count, frame_count, patch_count, width = inputs.shape
    clips, frames = lax.axis_size("clip"), lax.axis_size("frame")
    owners = clips * frames
    owner = lax.axis_index("clip") * frames + lax.axis_index("frame")
    part = patch_count // frames
    rows = ada_weight.shape[0]

    embed = jax.nn.silu(embed_steps(time_steps, width)).astype(bf16)
    embed = jnp.pad(embed, ((0, 16 - clip_count), (0, 0)))
    place = lax.broadcasted_iota(jnp.int32, (width, 128), 0) - owner * rows
    lane = lax.broadcasted_iota(jnp.int32, (width, 128), 1)
    select = ((place == lane) & (lane < rows)).astype(bf16)
    ada = jnp.pad(ada_weight, ((0, 128 - rows), (0, 0)))

    def spread_bias(vector):
        length = vector.shape[0]
        empty = jnp.zeros((owners * length,), f32)
        return lax.dynamic_update_slice(empty, vector.astype(f32), (owner * length,)).reshape(
            -1, width
        )

    bias = jnp.concatenate(
        [
            spread_bias(vector)
            for vector in (ada_bias, space_out_bias, time_out_bias, up_bias, down_bias)
        ],
        axis=0,
    )
    sh_c = jnp.concatenate([space_qkv, space_out], axis=1)
    sh_b = jnp.concatenate([time_qkv, time_out], axis=1)
    (
        w_c, w_b, w_u, w_d, mod, chosen, totals, hidden_one, qkv_one, mixed_one, branch_one,
        after_first, after_later, cot_first,
    ) = start_call(
        clips, frames, inputs, cotangent, sh_c, sh_b, up_weight, down_weight, embed, select, ada,
        bias,
    )

    def exchange(values):
        return lax.all_to_all(values, "frame", split_axis=0, concat_axis=0, tiled=True)

    loss = jnp.exp2(weight_index.astype(f32) * 0.5 - 1.0)
    loss = jnp.broadcast_to(loss[:, None], (clip_count, width))
    cots, afters = [cot_first], [after_first]
    for clip in range(1, clip_count):
        patches = cotangent[clip].reshape(frame_count, frames, part, width)
        cots.append(exchange(jnp.swapaxes(patches, 0, 1)))
        place = (clip - 1) * frame_count
        patches = after_later[place : place + frame_count]
        patches = patches.reshape(frame_count, frames, part, width)
        afters.append(exchange(jnp.swapaxes(patches, 0, 1)))

    earlier = None
    outs, grads, mid_sums = [], [], []
    for clip in range(clip_count):
        out, grad, *rest = middle_call(
            clip, clip_count, afters[clip], cots[clip], loss, mod, w_b, w_u, w_d, earlier
        )
        earlier = rest[:-1]
        mid_sums.append(rest[-1])
        outs.append(exchange(out))
        grads.append(exchange(grad))
    act, gup, h3, gb3, mixed_two, gb2, h2, gqkv_two = earlier
    grad_down = dot(act, gb3, 0, 0).astype(bf16)
    grad_up = dot(h3, gup, 0, 0).astype(bf16)
    grad_tout = dot(mixed_two, gb2, 0, 0).astype(bf16)
    grad_tqkv = dot(h2, gqkv_two, 0, 0).astype(bf16)

    earlier = None
    space_sums = []
    for clip in range(clip_count):
        *earlier, sums = space_back_call(
            clip, grads[clip], inputs, mod, w_c, qkv_one, branch_one, totals, earlier
        )
        space_sums.append(sums)
    input_grad, gb1, gqkv_one = earlier
    grad_sout = dot(mixed_one.reshape(-1, width), gb1, 0, 0).astype(bf16)
    grad_sqkv = dot(hidden_one.reshape(-1, width), gqkv_one, 0, 0).astype(bf16)

    pieces = []
    for clip in range(clip_count):
        pieces += [space_sums[clip][0:3], mid_sums[clip][0:6]]
    pieces.append(sum(entry[3:4] for entry in space_sums))
    pieces.append(sum(entry[6:12] for entry in mid_sums))
    small = jnp.concatenate(pieces, axis=0)
    small = jnp.pad(small, ((0, ROWS - small.shape[0]), (0, 0)))
    gathered = end_call(clips, frames, small)
    count = clip_count * 9
    grad_modulation = gathered[:, :count].reshape(clips * clip_count, 9 * width)
    picked = chosen.reshape(clips, 16, 128)[:, :clip_count, :rows].reshape(-1, rows)
    grad_ada = lax.dot_general(
        picked.astype(f32), grad_modulation, (((0,), (0,)), ((), ())), precision=highest
    )
    grad_ada_bias = jnp.sum(grad_modulation, axis=0)
    biases = jnp.sum(gathered[:, count : count + 7], axis=0)

    def own_slice(vector):
        length = vector.shape[0] // owners
        return lax.dynamic_slice_in_dim(vector, owner * length, length, 0)

    outputs = jnp.stack(
        [
            jnp.swapaxes(out, 0, 1).reshape(frame_count, patch_count, width)
            for out in outs
        ]
    )
    return (
        outputs,
        input_grad,
        grad_ada,
        own_slice(grad_ada_bias),
        scatter_rows(grad_sqkv),
        scatter_rows(grad_sout),
        own_slice(biases[0]),
        scatter_rows(grad_tqkv),
        scatter_rows(grad_tout),
        own_slice(biases[1]),
        scatter_rows(grad_up),
        own_slice(biases[2:6].reshape(-1)),
        scatter_rows(grad_down),
        own_slice(biases[6]),
    )


def solution(mesh):
    tokens = P("clip", "frame", None, None)
    matrix = P(("clip", "frame"), None)
    vector = P(("clip", "frame"))
    in_specs = (
        tokens, tokens, P("clip"), P("clip"), matrix, vector, matrix, matrix, vector, matrix,
        matrix, vector, matrix, vector, matrix, vector,
    )
    out_specs = (
        tokens, tokens, matrix, vector, matrix, matrix, vector, matrix, matrix, vector, matrix,
        vector, matrix, vector,
    )
    return jax.shard_map(shards, mesh=mesh, in_specs=in_specs, out_specs=out_specs, check_vma=False)
```

time: 1670 us -> 1030 us (0.62)
  Pallas kernels: 0 us -> 396 us
  matrix products: 410 us -> 69.7 us
  local copies, waits for them, and re-layouts: 266 us -> 25.5 us
  waiting for transfers between devices: 663 us -> 472 us
  blocking collectives: 176 us -> 0 us
  other arithmetic: 117 us -> 21.7 us
    pallas_call x0 -> x6, Pallas kernels: none -> 396 us  [the longest x2 157 us: middle_call(): pl.pallas_call(body, grid=(tiles,), in_specs=in_specs, out_specs=[block,...]
    dot_general x32 -> x7, matrix products: 410 us -> 69.7 us  [the longest x6 68.3 us: dot(): lax.dot_general(left, right, (((left_dim,), (right_dim,)), ((), ())), pre...]
    all_to_all x3 -> x6, waiting for transfers between devices: 214 us -> 59.8 us  [exchange(): lax.all_to_all(values, 'frame', split_axis=0, concat_axis=0, tiled=True)]
    reshape x19 -> x8, local copies, waits for them, and re-layouts: 156 us -> 4.7 us  [the longest x1 2.69 us: shards(): patches = patches.reshape(frame_count, frames, part, width)]
    all_gather x7 -> x0, waiting for transfers between devices: 94.5 us -> none  [the longest x1 55.1 us: shards(): lax.all_gather(space_qkv, ('clip', 'frame'), axis=0, tiled=True)]
    all_to_all x1 -> x0, blocking collectives: 93.3 us -> none  [shards(): lax.all_to_all(grad_patch_hidden, 'frame', split_axis=1, concat_axis=2, t...]
    convert_element_type x8 -> x0, local copies, waits for them, and re-layouts: 70.4 us -> none  [the longest x2 45.3 us: shards(): grad_qkv_two = jnp.swapaxes(grad_split_two, 1, 2).reshape(clip_count, fra...]
    reduce_scatter x7 -> x6, waiting for transfers between devices: 350 us -> 412 us  [scatter_rows(): lax.psum_scatter(grad, ('clip', 'frame'), scatter_dimension=0, tiled=True)]
  transfers between devices with their start and end apart: 17 -> 12, of which waited for: 8 -> 6; matrix products, arithmetic and copies ran while one was open for 42% -> 9% of each run, Pallas kernels for 0% -> 26%
where the time goes in v1:
time: 1030 us
  waiting for transfers between devices  472 us (46%)
  Pallas kernels  396 us (38%)
  matrix products  69.7 us (7%)
  starting transfers between devices  26.4 us (3%)
  local copies, waits for them, and re-layouts  25.5 us (2%)
  other arithmetic  21.7 us (2%)
  between operations  14.6 us (1%)
    reduce_scatter x6, waiting for transfers between devices, scatter_rows(): lax.psum_scatter(grad, ('clip', 'frame'), scatter_dimension=0, tiled=True)  412 us
    pallas_call x2, Pallas kernels, middle_call(): pl.pallas_call(body, grid=(tiles,), in_specs=in_specs, out_specs=[block,...  157 us
    pallas_call x1, Pallas kernels, start_call(): pl.pallas_call(functools.partial(start_kernel, clips, frames, clip_count)...  124 us
    dot_general x6, matrix products, dot(): lax.dot_general(left, right, (((left_dim,), (right_dim,)), ((), ())), pre...  68.3 us
    pallas_call x2, Pallas kernels, space_back_call(): pl.pallas_call(body, grid=(frame_count,), in_specs=in_specs, out_specs=[p...  63.8 us
    all_to_all x6, waiting for transfers between devices, exchange(): lax.all_to_all(values, 'frame', split_axis=0, concat_axis=0, tiled=True)  59.8 us
    pallas_call x1, Pallas kernels, end_call(): pl.pallas_call(functools.partial(end_kernel, clips, frames), out_shape=ja...  50.7 us
    all_to_all x6, starting transfers between devices, exchange(): lax.all_to_all(values, 'frame', split_axis=0, concat_axis=0, tiled=True)  26.2 us
  transfers between devices with their start and end apart: 12, of which 6 were waited for; matrix products, arithmetic and copies ran while one was open for 9% of the time, Pallas kernels for 26%

profile of v1, /device:TPU:0, one launch (start us, length us, event | category | flops | bytes accessed | tf_op | source)
XLA Modules:
  0.0 1026.2 jit_solution(8086881277750727700)
XLA Ops:
  12.2 2.3 pad.13.ada
  19.0 2.0 concatenate.18.bias
  21.0 124.4 %shard_map.263 = (bf16[768,3072]{1,0:T(8,128)(2,1)}, bf16[768,3072]{1,0:T(8,128)(2,1)}, bf16[768,3072]{1,0:T(8,128)(2,1)}, bf16[3072,768]{1,0:T(8,128)(2,1)}, f3...) custom-call(bf16[2,4,256,768]{3,2,1,0:T(8,128)(2,1)} %refs_1_.1, ...), custom_call_target="tpu_custom_call" | custom-call | tf_op jit(solution)/shard_map/pallas_call | solution.py:440
  145.4 2.7 copy.48
  148.0 3.7 all-to-all-start.1
  153.1 36.0 %all-to-all-done.1.refs_0_ = bf16[4,4,64,768]{3,2,1,0:T(8,128)(2,1)S(1)} async-done(((bf16[4,4,64,768]{3,2,1,0:T(8,128)(2,1)}), bf16[4,4,64,768]{3,2,1,0:T(8,128)(2,1)S(1)}, u32[]{:S(2)}, u32[]{:S(2)}) %all-to-all-start.1) | async-done | bytes 1572896 | tf_op jit(solution)/shard_map/all_to_all | solution.py:861
  189.0 3.6 all-to-all-start.2
  193.3 83.6 %shard_map.264 = (bf16[4,4,64,768]{3,2,1,0:T(8,128)(2,1)}, bf16[4,4,64,768]{3,2,1,0:T(8,128)(2,1)}, bf16[2048,3072]{1,0:T(8,128)(2,1)}, bf16[2048,3072]{1,0:T(8,...) custom-call(bf16[4,4,64,768]{3,2,1,0:T(8,128)(2,1)} %get-tuple-eleme, ...), custom_call_target="tpu_custom_call" | custom-call | flops 102400000000 | bytes 40960000 | tf_op jit(solution)/shard_map/pallas_call | solution.py:704
  278.0 5.1 all-to-all-start.5
  283.1 73.5 %shard_map.265 = (bf16[4,4,64,768]{3,2,1,0:T(8,128)(2,1)}, bf16[4,4,64,768]{3,2,1,0:T(8,128)(2,1)}, bf16[2048,3072]{1,0:T(8,128)(2,1)}, bf16[2048,3072]{1,0:T(8,...) custom-call(bf16[4,4,64,768]{3,2,1,0:T(8,128)(2,1)} %copy-done.3, ...), custom_call_target="tpu_custom_call", output_to_operand_aliasing={{2}: (7, {}), {3}: (8, {}), {4}: (9, {}), {5}: (10, {}), {6... | custom-call | flops 102400000000 | bytes 40960000 | tf_op jit(solution)/shard_map/pallas_call | solution.py:704
  356.7 5.1 all-to-all-start.4
  361.8 6.5 convolution_convert_fusion.4
  368.4 31.7 %shard_map.266 = (f32[2,4,256,768]{3,2,1,0:T(8,128)}, bf16[2048,768]{1,0:T(8,128)(2,1)}, bf16[2048,2304]{1,0:T(8,128)(2,1)}, f32[8,768]{1,0:T(8,128)}) custom-call(bf16[4,4,64,768]{3,2,1,0:T(8,128)(2,1)} %copy-done.2, bf16[2,4,256,768]{3,2,1,0:T(8,128)(2,1)} %refs_1_.1, f32[32,768]{1,0:T(8,128)} %get-tuple-element.60.mod.refs_3_.refs_2_, ...), custom_call_target="tpu_custom_call" | custom-call | flops 20480000000 | bytes 15728640 | tf_op jit(solution)/shard_map/pallas_call | solution.py:787
  401.3 32.1 %shard_map.267 = (f32[2,4,256,768]{3,2,1,0:T(8,128)}, bf16[2048,768]{1,0:T(8,128)(2,1)}, bf16[2048,2304]{1,0:T(8,128)(2,1)}, f32[8,768]{1,0:T(8,128)}) custom-call(bf16[4,4,64,768]{3,2,1,0:T(8,128)(2,1)} %copy-done.5, bf16[2,4,256,768]{3,2,1,0:T(8,128)(2,1)} %refs_1_.1, ...), custom_call_target="tpu_custom_call", output_to_operand_aliasing={{0}: (7, {}), {1}: (8, {}), {2}: (9, {})} | custom-call | flops 20480000000 | bytes 15728640 | tf_op jit(solution)/shard_map/pallas_call | solution.py:787
  433.4 5.6 convolution_convert_fusion.5
  439.1 13.6 %convolution_convert_fusion.2 = bf16[768,2304]{1,0:T(8,128)(2,1)} fusion(bf16[2048,768]{1,0:T(8,128)(2,1)} %get-tuple-element.94, bf16[2048,2304]{1,0:T(8,128)(2,1)} %get-tuple-element.95), kind=kOutput, calls=%fused_computation.2 | convolution fusion | flops 7249526784 | bytes 16121856 | tf_op jit(solution)/shard_map/dot_general | solution.py:37
  452.8 1.8 copy-done.13
  454.6 14.6 %convolution_convert_fusion = bf16[3072,768]{1,0:T(8,128)(2,1)} fusion(bf16[2048,3072]{1,0:T(8,128)(2,1)} %get-tuple-element.100, bf16[2048,768]{1,0:T(8,128)(2,1)S(1)} %copy-done.13), kind=kOutput, calls=%fused_computation | convolution fusion | flops 9666035712 | bytes 20447232 | tf_op jit(solution)/shard_map/dot_general | solution.py:37
  469.3 1.8 copy-done.12
  471.1 14.7 %convolution_convert_fusion.1 = bf16[768,3072]{1,0:T(8,128)(2,1)} fusion(bf16[2048,768]{1,0:T(8,128)(2,1)S(1)} %copy-done.12, bf16[2048,3072]{1,0:T(8,128)(2,1)} %get-tuple-element.99), kind=kOutput, calls=%fused_computation.1 | convolution fusion | flops 9666035712 | bytes 20447232 | tf_op jit(solution)/shard_map/dot_general | solution.py:37
  485.8 5.1 all-to-all-start
  491.0 13.3 %convolution_convert_fusion.3 = bf16[768,2304]{1,0:T(8,128)(2,1)} fusion(bf16[2048,768]{1,0:T(8,128)(2,1)} %bitcast.53, bf16[2048,2304]{1,0:T(8,128)(2,1)} %get-tuple-element.91), kind=kOutput, calls=%fused_computation.3 | convolution fusion | flops 7249526784 | bytes 16121856 | tf_op jit(solution)/shard_map/dot_general | solution.py:37
  504.3 23.8 %all-to-all-done = bf16[4,4,64,768]{3,2,1,0:T(8,128)(2,1)S(1)} async-done(((bf16[4,4,64,768]{3,2,1,0:T(8,128)(2,1)}), bf16[4,4,64,768]{3,2,1,0:T(8,128)(2,1)S(1)}, u32[]{:S(2)}, u32[]{:S(2)}) %all-to-all-start) | async-done | bytes 1572896 | tf_op jit(solution)/shard_map/all_to_all | solution.py:861
  528.1 3.7 all-to-all-start.3
  536.2 50.7 %shard_map.268 = f32[8,32,768]{2,1,0:T(8,128)} custom-call(f32[32,768]{1,0:T(8,128)} %pad.14.small), custom_call_target="tpu_custom_call" | custom-call | tf_op jit(solution)/shard_map/pallas_call | solution.py:509
  586.9 2.0 slice.58
  588.9 2.0 reshape.103
  595.6 1.9 pad_maximum_fusion
  600.3 86.1 %reduce-scatter.11.cloned.1.call-done = bf16[24,2304]{1,0:T(8,128)(2,1)} async-done(((bf16[768,2304]{1,0:T(8,128)(2,1)}), bf16[24,2304]{1,0:T(8,128)(2,1)}) %reduce-scatter.11.cloned.1.call-update) | async-done | bytes 110608 | tf_op jit(solution)/shard_map/reduce_scatter | solution.py:813
  688.0 109.7 %reduce-scatter.17.cloned.1.call-done = bf16[96,768]{1,0:T(8,128)(2,1)} async-done(((bf16[3072,768]{1,0:T(8,128)(2,1)}), bf16[96,768]{1,0:T(8,128)(2,1)}) %reduce-scatter.17.cloned.1.call-update) | async-done | bytes 147472 | tf_op jit(solution)/shard_map/reduce_scatter | solution.py:813
  799.4 110.7 %reduce-scatter.15.cloned.1.call-done = bf16[24,3072]{1,0:T(8,128)(2,1)} async-done(((bf16[768,3072]{1,0:T(8,128)(2,1)}), bf16[24,3072]{1,0:T(8,128)(2,1)}) %reduce-scatter.15.cloned.1.call-update) | async-done | bytes 147472 | tf_op jit(solution)/shard_map/reduce_scatter | solution.py:813
  911.7 105.8 %reduce-scatter.7.cloned.1.call-done = bf16[24,2304]{1,0:T(8,128)(2,1)} async-done(((bf16[768,2304]{1,0:T(8,128)(2,1)}), bf16[24,2304]{1,0:T(8,128)(2,1)}) %reduce-scatter.7.cloned.1.call-update) | async-done | bytes 110608 | tf_op jit(solution)/shard_map/reduce_scatter | solution.py:813
  (99 shorter events, 32.3 us)
Async XLA Ops:
  148.0 3.7 slice-start
  148.0 41.0 %all-to-all-start.1 = ((bf16[4,4,64,768]{3,2,1,0:T(8,128)(2,1)}), bf16[4,4,64,768]{3,2,1,0:T(8,128)(2,1)S(1)}, u32[]{:S(2)}, u32[]{:S(2)}) async-start(bf16[4,4,64,768]{3,2,1,0:T(8,128)(2,1)} %bitcast.44), calls=%async_computation.1 | async-start | bytes 3145728 | tf_op jit(solution)/shard_map/all_to_all | solution.py:861
  151.7 1.3 copy-start.11
  189.0 87.8 %copy-start.3 = (bf16[4,4,64,768]{3,2,1,0:T(8,128)(2,1)}, bf16[4,4,64,768]{3,2,1,0:T(8,128)(2,1)S(1)}, u32[]{:S(2)}) copy-start(bf16[4,4,64,768]{3,2,1,0:T(8,128)(2,1)S(1)} %all-to-all-done.1.refs_0_) | copy-start | bytes 4718596
  189.0 87.8 %all-to-all-start.2 = ((bf16[4,4,64,768]{3,2,1,0:T(8,128)(2,1)}), bf16[4,4,64,768]{3,2,1,0:T(8,128)(2,1)S(1)}, u32[]{:S(2)}, u32[]{:S(2)}) async-start(bf16[4,4,64,768]{3,2,1,0:T(8,128)(2,1)} %bitcast.43), calls=%async_computation.2 | async-start | bytes 3145728 | tf_op jit(solution)/shard_map/all_to_all | solution.py:861
  276.9 1.2 copy-start.4
  278.0 78.6 %all-to-all-start.5 = ((bf16[4,4,64,768]{3,2,1,0:T(8,128)(2,1)}), bf16[4,4,64,768]{3,2,1,0:T(8,128)(2,1)S(1)}, u32[]{:S(2)}, u32[]{:S(2)}) async-start(bf16[4,4,64,768]{3,2,1,0:T(8,128)(2,1)} %get-tuple-element.80), calls=%async_computation.5 | async-start | bytes 3145728 | tf_op jit(solution)/shard_map/all_to_all | solution.py:861
  356.6 11.7 %copy-start.2 = (bf16[4,4,64,768]{3,2,1,0:T(8,128)(2,1)}, bf16[4,4,64,768]{3,2,1,0:T(8,128)(2,1)S(1)}, u32[]{:S(2)}) copy-start(bf16[4,4,64,768]{3,2,1,0:T(8,128)(2,1)S(1)} %all-to-all-done.5.grad_ref) | copy-start | bytes 4718596
  356.7 43.5 %all-to-all-start.4 = ((bf16[4,4,64,768]{3,2,1,0:T(8,128)(2,1)}), bf16[4,4,64,768]{3,2,1,0:T(8,128)(2,1)S(1)}, u32[]{:S(2)}, u32[]{:S(2)}) async-start(bf16[4,4,64,768]{3,2,1,0:T(8,128)(2,1)} %get-tuple-element.75), calls=%async_computation.4 | async-start | bytes 3145728 | tf_op jit(solution)/shard_map/all_to_all | solution.py:861
  361.8 172.0 %reduce-scatter.13.cloned.1.call-start = ((), (), s32[]{:S(2)}) async-start(), calls=%async_computation.15 | async-start | bytes 1216512 | tf_op jit(solution)/shard_map/reduce_scatter | solution.py:813
  368.3 230.5 %reduce-scatter.9.cloned.1.call-start = ((), (), s32[]{:S(2)}) async-start(), calls=%async_computation.13 | async-start | bytes 1216512 | tf_op jit(solution)/shard_map/reduce_scatter | solution.py:813
  400.1 1.1 copy-start.5
  401.3 32.1 %copy-start.10 = (bf16[8,256,768]{2,1,0:T(8,128)(2,1)S(1)}, bf16[8,256,768]{2,1,0:T(8,128)(2,1)}, u32[]{:S(2)}) copy-start(bf16[8,256,768]{2,1,0:T(8,128)(2,1)} %get-tuple-element.92) | copy-start | bytes 9437188
  439.0 247.4 %reduce-scatter.11.cloned.1.call-start = ((), (), s32[]{:S(2)}) async-start(), calls=%async_computation.14 | async-start | bytes 3649536 | tf_op jit(solution)/shard_map/reduce_scatter | solution.py:813
  452.7 1.9 copy-start.13
  452.8 345.0 %reduce-scatter.17.cloned.1.call-start = ((), (), s32[]{:S(2)}) async-start(), calls=%async_computation.17 | async-start | bytes 4866048 | tf_op jit(solution)/shard_map/reduce_scatter | solution.py:813
  469.2 1.9 copy-start.12
  469.2 440.8 %reduce-scatter.15.cloned.1.call-start = ((), (), s32[]{:S(2)}) async-start(), calls=%async_computation.16 | async-start | bytes 4866048 | tf_op jit(solution)/shard_map/reduce_scatter | solution.py:813
  485.8 42.2 %all-to-all-start = ((bf16[4,4,64,768]{3,2,1,0:T(8,128)(2,1)}), bf16[4,4,64,768]{3,2,1,0:T(8,128)(2,1)S(1)}, u32[]{:S(2)}, u32[]{:S(2)}) async-start(bf16[4,4,64,768]{3,2,1,0:T(8,128)(2,1)} %get-tuple-element.64), calls=%async_computation | async-start | bytes 3145728 | tf_op jit(solution)/shard_map/all_to_all | solution.py:861
  491.0 526.6 %reduce-scatter.7.cloned.1.call-start = ((), (), s32[]{:S(2)}) async-start(), calls=%async_computation.12 | async-start | bytes 3649536 | tf_op jit(solution)/shard_map/reduce_scatter | solution.py:813
  504.2 28.2 %copy-start.8 = (f32[8,768]{1,0:T(8,128)S(1)}, f32[8,768]{1,0:T(8,128)}, u32[]{:S(2)}) copy-start(f32[8,768]{1,0:T(8,128)} %get-tuple-element.86) | copy-start | bytes 73732
  528.0 5.7 copy-start.6
  528.0 5.7 copy-start.7
  528.1 7.2 copy-start.9
  528.1 66.3 %all-to-all-start.3 = ((bf16[4,4,64,768]{3,2,1,0:T(8,128)(2,1)}), bf16[4,4,64,768]{3,2,1,0:T(8,128)(2,1)S(1)}, u32[]{:S(2)}, u32[]{:S(2)}) async-start(bf16[4,4,64,768]{3,2,1,0:T(8,128)(2,1)} %get-tuple-element.74), calls=%async_computation.3 | async-start | bytes 3145728 | tf_op jit(solution)/shard_map/all_to_all | solution.py:861
  586.9 8.7 copy-start
  595.6 1.9 copy-start.1
Sparse Core Ops, SparseCore 0:
  368.5 96.8 reduce-scatter.12
  470.5 108.5 reduce-scatter.8
  584.5 101.8 reduce-scatter.10
  691.7 105.9 reduce-scatter.16
  803.9 106.0 reduce-scatter.14
  915.4 102.1 reduce-scatter.6

commit v2 on v1

--- a/solution.py
+++ b/solution.py
@@ -485,40 +485,286 @@
     )(inputs, cotangent, sh_c, sh_b, sh_u, sh_d, embed, select, ada, bias)
 
 
-def end_kernel(clips, frames, small, out, lined, held, fs, fr, ps, pr):
+STEP = 256
+
+
+def grad_kernel(
+    clips, frames,
+    small, h3, gup, act, gb3, h2, gqkv2, mix2, gb2, h1, gqkv1, mix1, gb1,
+    gathered, out_u, out_d, out_b, out_c,
+    sum_w, sum_d, core_w, core_d, side_w, side_d, line_w, line_d, last_w, last_d,
+    left, right, total, lined, held,
+    lsem, rsem, cs, cr, xs, xr, zs, zr, fs, fr, ps, pr,
+):
     clip, frame = lax.axis_index("clip"), lax.axis_index("frame")
+    tokens = h3.shape[0]
+    width = small.shape[1]
+    wide = sum_w.shape[-1]
+    narrow = sum_d.shape[-1]
+    tail = clip_tail_masks(clips)
+    orders = (tail, tail[::-1])
+    masks = frame_masks(frames)
     greet(clips, frames)
     first = spread("frame", frames, lambda peer: small, lined, fs, fr)
     lined[frame] = small[...]
-    for copy in first:
-        copy.wait_recv()
-    total = lined[0]
-    for peer in range(1, frames):
-        total = total + lined[peer]
-    held[...] = total
-    second = spread("clip", clips, lambda peer: held, out, ps, pr)
-    out[clip] = total
+
+    chunks = [
+        (1, 0, [(act, gb3, 0, 0, narrow)], out_d, 0),
+        (1, 1, [(act, gb3, narrow, 0, narrow)], out_d, narrow),
+        (0, 0, [(h3, gup, 0, 0, wide)], out_u, 0),
+        (0, 1, [(h3, gup, wide, 0, wide)], out_u, wide),
+        (0, 2, [(h2, gqkv2, 0, 0, wide)], out_b, 0),
+        (0, 3, [(h2, gqkv2, wide, 0, width), (mix2, gb2, 0, width, width)], out_b, wide),
+        (0, 4, [(h1, gqkv1, 0, 0, wide)], out_c, 0),
+        (0, 5, [(h1, gqkv1, wide, 0, width), (mix1, gb1, 0, width, width)], out_c, wide),
+    ]
+    sums, cores, sides = (sum_w, sum_d), (core_w, core_d), (side_w, side_d)
+    lines, lasts = (line_w, line_d), (last_w, last_d)
+    flights = {}
+
+    def multiply(number):
+        kind, place, parts, _, _ = chunks[number]
+        for one, other, begin, at, lanes in parts:
+            height = one.shape[1]
+
+            def load(step, slot):
+                rows = pl.ds(pl.multiple_of(step * STEP, STEP), STEP)
+                return (
+                    pltpu.make_async_copy(
+                        one.at[rows, :], left.at[slot, :, pl.ds(0, height)], lsem.at[slot]
+                    ),
+                    pltpu.make_async_copy(
+                        other.at[rows, pl.ds(begin, lanes)],
+                        right.at[slot, :, pl.ds(0, lanes)],
+                        rsem.at[slot],
+                    ),
+                )
+
+            for copy in load(0, 0):
+                copy.start()
+            steps = tokens // STEP
+
+            def body(step, carry):
+                slot = lax.rem(step, 2)
+
+                @pl.when(step + 1 < steps)
+                def _():
+                    for copy in load(step + 1, lax.rem(step + 1, 2)):
+                        copy.start()
+
+                for copy in load(step, slot):
+                    copy.wait()
+                for group in range(height // width):
+                    rows = slice(group * width, (group + 1) * width)
+                    columns = slice(at + group * lanes, at + (group + 1) * lanes)
+                    product = dot(left[slot, :, rows], right[slot, :, :lanes], 0, 0)
+
+                    @pl.when(step == 0)
+                    def _():
+                        total[:, columns] = product
+
+                    @pl.when(step > 0)
+                    def _():
+                        total[:, columns] += product
+
+                return carry
+
+            lax.fori_loop(0, steps, body, 0)
+        rows, lanes = sums[kind].shape[2:]
+        for block in range(clips):
+            begin = block * rows
+            column = begin // width * lanes
+            begin = begin % width
+            sums[kind][place, block] = total[begin : begin + rows, column : column + lanes].astype(
+                bf16
+            )
+
+    def core_start(number):
+        kind, place = chunks[number][:2]
+        copies = []
+        for position, offset in enumerate(span(tail)):
+            copy = pltpu.make_async_remote_copy(
+                src_ref=sums[kind].at[place, flip(clip, offset ^ 1)],
+                dst_ref=cores[kind].at[place, position],
+                send_sem=cs.at[number, position],
+                recv_sem=cr.at[number, position],
+                device_id={"clip": flip(clip, 1)},
+                device_id_type=MESH,
+            )
+            copy.start()
+            copies.append(copy)
+        flights[number, "core"] = copies
+
+    def half_of(kind, half):
+        if kind:
+            rows = sums[kind].shape[2] // 2
+            return (slice(half * rows, (half + 1) * rows), slice(None))
+        lanes = sums[kind].shape[3] // 2
+        return (slice(None), slice(half * lanes, (half + 1) * lanes))
+
+    def side_start(number, step):
+        kind, place = chunks[number][:2]
+        copies = []
+        for half in range(2):
+            mask = orders[half][step]
+            for position, offset in enumerate(span(orders[half][:step])):
+                entry = (1 << step) - 1 + position
+                copy = pltpu.make_async_remote_copy(
+                    src_ref=sums[kind].at[(place, flip(clip, offset ^ mask)) + half_of(kind, half)],
+                    dst_ref=sides[kind].at[place, half, entry],
+                    send_sem=xs.at[number, half, entry],
+                    recv_sem=xr.at[number, half, entry],
+                    device_id={"clip": flip(clip, mask)},
+                    device_id_type=MESH,
+                )
+                copy.start()
+                copies.append(copy)
+        flights[number, "side", step] = copies
+
+    def core_add(number):
+        kind, place = chunks[number][:2]
+        for copy in flights[number, "core"]:
+            copy.wait_recv()
+        for position, offset in enumerate(span(tail)):
+            block = flip(clip, offset)
+            sums[kind][place, block] = (
+                sums[kind][place, block].astype(f32) + cores[kind][place, position].astype(f32)
+            ).astype(bf16)
+        side_start(number, len(tail) - 1)
+
+    def side_add(number, step):
+        kind, place = chunks[number][:2]
+        for copy in flights[number, "side", step]:
+            copy.wait_recv()
+        for half in range(2):
+            for position, offset in enumerate(span(orders[half][:step])):
+                entry = (1 << step) - 1 + position
+                block = flip(clip, offset)
+                where = (place, block) + half_of(kind, half)
+                sums[kind][where] = (
+                    sums[kind][where].astype(f32) + sides[kind][place, half, entry].astype(f32)
+                ).astype(bf16)
+        if step:
+            side_start(number, step - 1)
+        else:
+            rows = lines[kind].shape[2]
+            block = sums[kind][place, clip].astype(f32)
+            for slot in range(frames):
+                lines[kind][place, slot] = block[slot * rows : (slot + 1) * rows, :].astype(bf16)
+            line_start(number, len(masks) - 1)
+
+    def line_start(number, step):
+        kind, place = chunks[number][:2]
+        copies = []
+        for position, offset in enumerate(span(masks[:step])):
+            entry = (1 << step) - 1 + position
+            copy = pltpu.make_async_remote_copy(
+                src_ref=lines[kind].at[place, flip(frame, offset ^ masks[step])],
+                dst_ref=lasts[kind].at[place, entry],
+                send_sem=zs.at[number, entry],
+                recv_sem=zr.at[number, entry],
+                device_id={"frame": flip(frame, masks[step])},
+                device_id_type=MESH,
+            )
+            copy.start()
+            copies.append(copy)
+        flights[number, "line", step] = copies
+
+    def line_add(number, step):
+        kind, place, _, target, begin = chunks[number]
+        for copy in flights[number, "line", step]:
+            copy.wait_recv()
+        for position, offset in enumerate(span(masks[:step])):
+            entry = (1 << step) - 1 + position
+            slot = flip(frame, offset)
+            value = lines[kind][place, slot].astype(f32) + lasts[kind][place, entry].astype(f32)
+            if step:
+                lines[kind][place, slot] = value.astype(bf16)
+            else:
+                target[:, begin : begin + value.shape[1]] = value
+        if step:
+            line_start(number, step - 1)
+
+    stages = [core_start, core_add]
+    for step in range(len(tail))[::-1]:
+        stages.append(functools.partial(side_add, step=step))
+    for step in range(len(masks))[::-1]:
+        stages.append(functools.partial(line_add, step=step))
+
+    second = None
+    for turn in range(len(chunks) + len(stages) - 1):
+        for depth in range(len(stages))[::-1]:
+            if depth > 0 and 0 <= turn - depth < len(chunks):
+                stages[depth](turn - depth)
+        if turn < len(chunks):
+            multiply(turn)
+            core_start(turn)
+        if turn == 0:
+            for copy in first:
+                copy.wait_recv()
+            summed = lined[0]
+            for peer in range(1, frames):
+                summed = summed + lined[peer]
+            held[...] = summed
+            second = spread("clip", clips, lambda peer: held, gathered, ps, pr)
+            gathered[clip] = summed
     for copy in second:
         copy.wait_recv()
     for copy in first + second:
         copy.wait_send()
-
-
-def end_call(clips, frames, small):
+    for copies in flights.values():
+        for copy in copies:
+            copy.wait_send()
+
+
+def grad_call(clips, frames, small, *operands):
+    h3, gup, act = operands[:3]
+    width, hidden = h3.shape[1], act.shape[1]
+    owners = clips * frames
+    wide, narrow = hidden // 2, width // 2
+    rows_w, rows_d = width // owners, hidden // owners
+    peers = max(clips // 2 - 1, 1)
     vmem = pl.BlockSpec(memory_space=VMEM)
+    hbm = pl.BlockSpec(memory_space=pl.ANY)
+
     return pl.pallas_call(
-        functools.partial(end_kernel, clips, frames),
-        out_shape=jax.ShapeDtypeStruct((clips,) + small.shape, f32),
-        in_specs=[vmem],
-        out_specs=vmem,
+        functools.partial(grad_kernel, clips, frames),
+        out_shape=(
+            jax.ShapeDtypeStruct((clips,) + small.shape, f32),
+            jax.ShapeDtypeStruct((rows_w, hidden), f32),
+            jax.ShapeDtypeStruct((rows_d, width), f32),
+            jax.ShapeDtypeStruct((rows_w, hidden), f32),
+            jax.ShapeDtypeStruct((rows_w, hidden), f32),
+        ),
+        in_specs=[vmem] + [hbm] * len(operands),
+        out_specs=(vmem,) * 5,
         scratch_shapes=[
+            VMEM((6, clips, rows_w * frames, wide), bf16),
+            VMEM((2, clips, rows_d * frames, narrow), bf16),
+            VMEM((6, clips // 2, rows_w * frames, wide), bf16),
+            VMEM((2, clips // 2, rows_d * frames, narrow), bf16),
+            VMEM((6, 2, peers, rows_w * frames, wide // 2), bf16),
+            VMEM((2, 2, peers, rows_d * frames // 2, narrow), bf16),
+            VMEM((6, frames, rows_w, wide), bf16),
+            VMEM((2, frames, rows_d, narrow), bf16),
+            VMEM((6, frames - 1, rows_w, wide), bf16),
+            VMEM((2, frames - 1, rows_d, narrow), bf16),
+            VMEM((2, STEP, hidden), bf16),
+            VMEM((2, STEP, wide), bf16),
+            VMEM((width, wide), f32),
             VMEM((frames,) + small.shape, f32),
             VMEM(small.shape, f32),
+            DMA((2,)), DMA((2,)),
+            DMA((8, clips // 2)), DMA((8, clips // 2)),
+            DMA((8, 2, peers)), DMA((8, 2, peers)),
+            DMA((8, frames - 1)), DMA((8, frames - 1)),
             DMA((frames - 1,)), DMA((frames - 1,)),
             DMA((clips - 1,)), DMA((clips - 1,)),
         ],
-        compiler_params=pltpu.CompilerParams(collective_id=1, has_side_effects=True),
-    )(small)
+        compiler_params=pltpu.CompilerParams(
+            collective_id=1, has_side_effects=True, vmem_limit_bytes=VMEM_LIMIT
+        ),
+    )(small, *operands)
 
 
 def normed(values):
@@ -809,12 +1055,6 @@
     )(*args)
 
 
-def scatter_rows(grad):
-    return lax.psum_scatter(
-        grad, ("clip", "frame"), scatter_dimension=0, tiled=True
-    ).astype(f32)
-
-
 def shards(
     inputs, cotangent, time_steps, weight_index, ada_weight, ada_bias, space_qkv, space_out,
     space_out_bias, time_qkv, time_out, time_out_bias, up_weight, up_bias, down_weight, down_bias,
@@ -882,10 +1122,6 @@
         outs.append(exchange(out))
         grads.append(exchange(grad))
     act, gup, h3, gb3, mixed_two, gb2, h2, gqkv_two = earlier
-    grad_down = dot(act, gb3, 0, 0).astype(bf16)
-    grad_up = dot(h3, gup, 0, 0).astype(bf16)
-    grad_tout = dot(mixed_two, gb2, 0, 0).astype(bf16)
-    grad_tqkv = dot(h2, gqkv_two, 0, 0).astype(bf16)
 
     earlier = None
     space_sums = []
@@ -895,9 +1131,6 @@
         )
         space_sums.append(sums)
     input_grad, gb1, gqkv_one = earlier
-    grad_sout = dot(mixed_one.reshape(-1, width), gb1, 0, 0).astype(bf16)
-    grad_sqkv = dot(hidden_one.reshape(-1, width), gqkv_one, 0, 0).astype(bf16)
-
     pieces = []
     for clip in range(clip_count):
         pieces += [space_sums[clip][0:3], mid_sums[clip][0:6]]
@@ -905,7 +1138,11 @@
     pieces.append(sum(entry[6:12] for entry in mid_sums))
     small = jnp.concatenate(pieces, axis=0)
     small = jnp.pad(small, ((0, ROWS - small.shape[0]), (0, 0)))
-    gathered = end_call(clips, frames, small)
+    gathered, own_u, own_d, own_b, own_c = grad_call(
+        clips, frames, small, h3, gup, act, gb3, h2, gqkv_two, mixed_two, gb2,
+        hidden_one.reshape(-1, width), gqkv_one, mixed_one.reshape(-1, width), gb1,
+    )
+    cut = 3 * width
     count = clip_count * 9
     grad_modulation = gathered[:, :count].reshape(clips * clip_count, 9 * width)
     picked = chosen.reshape(clips, 16, 128)[:, :clip_count, :rows].reshape(-1, rows)
@@ -930,15 +1167,15 @@
         input_grad,
         grad_ada,
         own_slice(grad_ada_bias),
-        scatter_rows(grad_sqkv),
-        scatter_rows(grad_sout),
+        own_c[:, :cut],
+        own_c[:, cut:],
         own_slice(biases[0]),
-        scatter_rows(grad_tqkv),
-        scatter_rows(grad_tout),
+        own_b[:, :cut],
+        own_b[:, cut:],
         own_slice(biases[1]),
-        scatter_rows(grad_up),
+        own_u,
         own_slice(biases[2:6].reshape(-1)),
-        scatter_rows(grad_down),
+        own_d,
         own_slice(biases[6]),
     )
 

time: 1030 us -> 661 us (0.64)
  waiting for transfers between devices: 472 us -> 38.2 us
  Pallas kernels: 396 us -> 506 us
  matrix products: 69.7 us -> 2.33 us
  blocking collectives: 0 us -> 41 us
  between operations: 14.6 us -> 1.15 us
    reduce_scatter x6 -> x0, waiting for transfers between devices: 412 us -> none  [scatter_rows(): lax.psum_scatter(grad, ('clip', 'frame'), scatter_dimension=0, tiled=True)]
    pallas_call x1, Pallas kernels: 50.7 us -> 171 us  [grad_call(): pl.pallas_call(functools.partial(grad_kernel, clips, frames), out_shape=(...]
    dot_general x6 -> x0, matrix products: 68.3 us -> none  [dot(): lax.dot_general(left, right, (((left_dim,), (right_dim,)), ((), ())), pre...]
    all_to_all x0 -> x1, blocking collectives: none -> 41 us  [exchange(): lax.all_to_all(values, 'frame', split_axis=0, concat_axis=0, tiled=True)]
    all_to_all x6 -> x5, waiting for transfers between devices: 59.8 us -> 38.2 us  [exchange(): lax.all_to_all(values, 'frame', split_axis=0, concat_axis=0, tiled=True)]
    all_to_all x6 -> x5, starting transfers between devices: 26.2 us -> 19.4 us  [exchange(): lax.all_to_all(values, 'frame', split_axis=0, concat_axis=0, tiled=True)]
  transfers between devices with their start and end apart: 12 -> 5, of which waited for: 6 -> 2; matrix products, arithmetic and copies ran while one was open for 9% -> 2% of each run, Pallas kernels for 26% -> 59%
where the time goes in v2:
time: 661 us; the launch traced here: 651 us
  Pallas kernels  506 us (77%)
  blocking collectives  41 us (6%)
  waiting for transfers between devices  38.2 us (6%)
  local copies, waits for them, and re-layouts  29.9 us (5%)
  starting transfers between devices  19.4 us (3%)
  other arithmetic  13.1 us (2%)
    pallas_call x1, Pallas kernels, grad_call(): pl.pallas_call(functools.partial(grad_kernel, clips, frames), out_shape=(...  171 us
    pallas_call x2, Pallas kernels, middle_call(): pl.pallas_call(body, grid=(tiles,), in_specs=in_specs, out_specs=[block,...  147 us
    pallas_call x1, Pallas kernels, start_call(): pl.pallas_call(functools.partial(start_kernel, clips, frames, clip_count)...  124 us
    pallas_call x2, Pallas kernels, space_back_call(): pl.pallas_call(body, grid=(frame_count,), in_specs=in_specs, out_specs=[p...  63.5 us
    all_to_all x1, blocking collectives, exchange(): lax.all_to_all(values, 'frame', split_axis=0, concat_axis=0, tiled=True)  41 us
    all_to_all x5, waiting for transfers between devices, exchange(): lax.all_to_all(values, 'frame', split_axis=0, concat_axis=0, tiled=True)  38.2 us
    all_to_all x5, starting transfers between devices, exchange(): lax.all_to_all(values, 'frame', split_axis=0, concat_axis=0, tiled=True)  19.4 us
  transfers between devices with their start and end apart: 5, of which 2 were waited for; matrix products, arithmetic and copies ran while one was open for 2% of the time, Pallas kernels for 59%

profile of v2, /device:TPU:0, one launch (start us, length us, event | category | flops | bytes accessed | tf_op | source)
XLA Modules:
  0.0 651.1 jit_solution(14196803882185006954)
XLA Ops:
  2.1 2.3 pad.13.ada
  7.9 1.6 pad_maximum_fusion.1.sh_c
  9.5 1.6 pad_maximum_fusion.2.sh_b
  12.4 2.0 concatenate.18.bias
  14.4 124.4 %shard_map.263 = (bf16[768,3072]{1,0:T(8,128)(2,1)}, bf16[768,3072]{1,0:T(8,128)(2,1)}, bf16[768,3072]{1,0:T(8,128)(2,1)}, bf16[3072,768]{1,0:T(8,128)(2,1)}, f3...) custom-call(bf16[2,4,256,768]{3,2,1,0:T(8,128)(2,1)} %refs_1_.1, ...), custom_call_target="tpu_custom_call" | custom-call | tf_op jit(solution)/shard_map/pallas_call | solution.py:440
  138.8 2.7 copy.48
  141.5 3.7 all-to-all-start.1
  145.2 1.3 copy.47
  146.5 36.0 %all-to-all-done.1.refs_0_ = bf16[4,4,64,768]{3,2,1,0:T(8,128)(2,1)S(1)} async-done(((bf16[4,4,64,768]{3,2,1,0:T(8,128)(2,1)}), bf16[4,4,64,768]{3,2,1,0:T(8,128)(2,1)S(1)}, u32[]{:S(2)}, u32[]{:S(2)}) %all-to-all-start.1) | async-done | bytes 1572896 | tf_op jit(solution)/shard_map/all_to_all | solution.py:1101
  182.5 3.6 all-to-all-start.2
  186.7 73.4 %shard_map.264 = (bf16[4,4,64,768]{3,2,1,0:T(8,128)(2,1)}, bf16[4,4,64,768]{3,2,1,0:T(8,128)(2,1)}, bf16[2048,3072]{1,0:T(8,128)(2,1)}, bf16[2048,3072]{1,0:T(8,...) custom-call(bf16[4,4,64,768]{3,2,1,0:T(8,128)(2,1)} %get-tuple-eleme, ...), custom_call_target="tpu_custom_call" | custom-call | flops 102400000000 | bytes 40960000 | tf_op jit(solution)/shard_map/pallas_call | solution.py:950
  260.1 1.1 copy-done.3
  261.3 41.0 %all_to_all.30 = bf16[4,4,64,768]{3,2,1,0:T(8,128)(2,1)S(1)} all-to-all(bf16[4,4,64,768]{3,2,1,0:T(8,128)(2,1)} %get-tuple-element.69), channel_id=1, replica_groups=mesh['clip'=8,'frame'=4] {'frame'}, dimensions={0} | all-to-all | bytes 3145728 | tf_op jit(solution)/shard_map/all_to_all | solution.py:1101
  302.3 3.6 all-to-all-start.5
  305.8 73.6 %shard_map.265 = (bf16[4,4,64,768]{3,2,1,0:T(8,128)(2,1)}, bf16[4,4,64,768]{3,2,1,0:T(8,128)(2,1)}, bf16[2048,3072]{1,0:T(8,128)(2,1)}, bf16[2048,3072]{1,0:T(8,...) custom-call(bf16[4,4,64,768]{3,2,1,0:T(8,128)(2,1)} %copy-done.1, ...), custom_call_target="tpu_custom_call", output_to_operand_aliasing={{2}: (7, {}), {3}: (8, {}), {4}: (9, {}), {5}: (10, {}), {6... | custom-call | flops 102400000000 | bytes 40960000 | tf_op jit(solution)/shard_map/pallas_call | solution.py:950
  379.4 5.0 all-to-all-start.4
  385.4 31.7 %shard_map.266 = (f32[2,4,256,768]{3,2,1,0:T(8,128)}, bf16[2048,768]{1,0:T(8,128)(2,1)}, bf16[2048,2304]{1,0:T(8,128)(2,1)}, f32[8,768]{1,0:T(8,128)}) custom-call(bf16[4,4,64,768]{3,2,1,0:T(8,128)(2,1)} %copy-done.2, bf16[2,4,256,768]{3,2,1,0:T(8,128)(2,1)} %refs_1_.1, f32[32,768]{1,0:T(8,128)} %get-tuple-element.65.mod.refs_3_.refs_2_, ...), custom_call_target="tpu_custom_call" | custom-call | flops 20480000000 | bytes 15728640 | tf_op jit(solution)/shard_map/pallas_call | solution.py:1033
  417.8 2.3 all-to-all-done.4.refs_0_
  420.1 3.6 all-to-all-start.3
  423.7 31.8 %shard_map.267 = (f32[2,4,256,768]{3,2,1,0:T(8,128)}, bf16[2048,768]{1,0:T(8,128)(2,1)}, bf16[2048,2304]{1,0:T(8,128)(2,1)}, f32[8,768]{1,0:T(8,128)}) custom-call(bf16[4,4,64,768]{3,2,1,0:T(8,128)(2,1)} %all-to-all-done.4.refs_0_, bf16[2,4,256,768]{3,2,1,0:T(8,128)(2,1)} %refs_1_.1, ...), custom_call_target="tpu_custom_call", output_to_operand_aliasing={{0}: (7, {}), {1}: (8, {}), {2}: (9, {})} | custom-call | flops 20480000000 | bytes 15728640 | tf_op jit(solution)/shard_map/pallas_call | solution.py:1033
  458.0 171.1 %shard_map.268 = (f32[8,32,768]{2,1,0:T(8,128)}, f32[24,3072]{1,0:T(8,128)}, f32[96,768]{1,0:T(8,128)}, f32[24,3072]{1,0:T(8,128)}, f32[24,3072]{1,0:T(8,128)}) custom-call(f32[32,768]{1,0:T(8,128)} %pad.14.small, bf16[2048,768]{1,0:T(8,128)(2,1)} %get-tuple-element.95.h3, bf16[2048,3072]{1,0:T(8,128)(2,1)} %get-tuple-element.96.gup, ...), custom_call_target="tpu_custom_call" | custom-call | tf_op jit(solution)/shard_map/pallas_call | solution.py:730
  629.0 1.6 slice.71
  630.7 1.5 slice.72
  632.2 1.6 slice.75
  633.8 1.5 slice.76
  635.4 1.9 slice.70
  637.3 1.0 slice_reduce_fusion
  638.3 1.3 copy.44
  639.6 2.1 reshape.105
  641.7 2.3 fusion.7
  644.0 1.1 reduce_sum.18
  646.9 1.9 pad_maximum_fusion
  (64 shorter events, 14.9 us)
Async XLA Ops:
  141.5 3.7 slice-start
  141.5 41.0 %all-to-all-start.1 = ((bf16[4,4,64,768]{3,2,1,0:T(8,128)(2,1)}), bf16[4,4,64,768]{3,2,1,0:T(8,128)(2,1)S(1)}, u32[]{:S(2)}, u32[]{:S(2)}) async-start(bf16[4,4,64,768]{3,2,1,0:T(8,128)(2,1)} %bitcast.32), calls=%async_computation.1 | async-start | bytes 3145728 | tf_op jit(solution)/shard_map/all_to_all | solution.py:1101
  145.2 1.3 copy-start.8
  182.5 77.6 %copy-start.1 = (bf16[4,4,64,768]{3,2,1,0:T(8,128)(2,1)}, bf16[4,4,64,768]{3,2,1,0:T(8,128)(2,1)S(1)}, u32[]{:S(2)}) copy-start(bf16[4,4,64,768]{3,2,1,0:T(8,128)(2,1)S(1)} %all-to-all-done.1.refs_0_) | copy-start | bytes 4718596
  182.5 77.6 %all-to-all-start.2 = ((bf16[4,4,64,768]{3,2,1,0:T(8,128)(2,1)}), bf16[4,4,64,768]{3,2,1,0:T(8,128)(2,1)S(1)}, u32[]{:S(2)}, u32[]{:S(2)}) async-start(bf16[4,4,64,768]{3,2,1,0:T(8,128)(2,1)} %bitcast.31), calls=%async_computation.2 | async-start | bytes 3145728 | tf_op jit(solution)/shard_map/all_to_all | solution.py:1101
  260.1 1.2 copy-start.3
  302.3 77.1 %all-to-all-start.5 = ((bf16[4,4,64,768]{3,2,1,0:T(8,128)(2,1)}), bf16[4,4,64,768]{3,2,1,0:T(8,128)(2,1)S(1)}, u32[]{:S(2)}, u32[]{:S(2)}) async-start(bf16[4,4,64,768]{3,2,1,0:T(8,128)(2,1)} %get-tuple-element.85), calls=%async_computation.5 | async-start | bytes 3145728 | tf_op jit(solution)/shard_map/all_to_all | solution.py:1101
  379.4 5.8 copy-start.2
  379.4 40.7 %all-to-all-start.4 = ((bf16[4,4,64,768]{3,2,1,0:T(8,128)(2,1)}), bf16[4,4,64,768]{3,2,1,0:T(8,128)(2,1)}, u32[]{:S(2)}, u32[]{:S(2)}) async-start(bf16[4,4,64,768]{3,2,1,0:T(8,128)(2,1)} %get-tuple-element.80), calls=%async_computation.4 | async-start | bytes 3145728 | tf_op jit(solution)/shard_map/all_to_all | solution.py:1101
  385.3 32.5 %copy-start.6 = (f32[16,768]{1,0:T(8,128)S(1)}, f32[16,768]{1,0:T(8,128)}, u32[]{:S(2)}) copy-start(f32[16,768]{1,0:T(8,128)} %get-tuple-element.92) | copy-start | bytes 147460
  385.4 32.5 %copy-start.7 = (f32[16,768]{1,0:T(8,128)S(1)}, f32[16,768]{1,0:T(8,128)}, u32[]{:S(2)}) copy-start(f32[16,768]{1,0:T(8,128)} %get-tuple-element.94) | copy-start | bytes 147460
  420.1 218.2 %all-to-all-start.3 = ((bf16[4,4,64,768]{3,2,1,0:T(8,128)(2,1)}), bf16[4,4,64,768]{3,2,1,0:T(8,128)(2,1)S(1)}, u32[]{:S(2)}, u32[]{:S(2)}) async-start(bf16[4,4,64,768]{3,2,1,0:T(8,128)(2,1)} %get-tuple-element.79), calls=%async_computation.3 | async-start | bytes 3145728 | tf_op jit(solution)/shard_map/all_to_all | solution.py:1101
  639.6 7.3 %copy-start = (bf16[4,4,64,768]{3,2,1,0:T(8,128)(2,1)S(1)}, bf16[4,4,64,768]{3,2,1,0:T(8,128)(2,1)}, u32[]{:S(2)}) copy-start(bf16[4,4,64,768]{3,2,1,0:T(8,128)(2,1)} %copy.44) | copy-start | bytes 4718596
  646.9 2.5 copy-start.5
  646.9 3.2 copy-start.4

commit v3 on v2

--- a/solution.py
+++ b/solution.py
@@ -485,7 +485,8 @@
     )(inputs, cotangent, sh_c, sh_b, sh_u, sh_d, embed, select, ada, bias)
 
 
-STEP = 256
+STEP = 512
+SLOTS = 3
 
 
 def grad_kernel(
@@ -522,50 +523,66 @@
     lines, lasts = (line_w, line_d), (last_w, last_d)
     flights = {}
 
+    steps = tokens // STEP
+    line_up = []
+    for kind, _, parts, _, _ in chunks:
+        for part in parts:
+            for group in range(part[0].shape[1] // width):
+                line_up.append(part[:3] + (part[3] + group * part[4], part[4], group))
+    begins = [0]
+    for kind, _, parts, _, _ in chunks:
+        begins.append(begins[-1] + sum(part[0].shape[1] // width for part in parts))
+
+    def load(entry, step, slot):
+        one, other, begin, _, lanes, group = line_up[entry]
+        rows = pl.ds(pl.multiple_of(step * STEP, STEP), STEP)
+        return (
+            pltpu.make_async_copy(
+                one.at[rows, pl.ds(group * width, width)], left.at[slot], lsem.at[slot]
+            ),
+            pltpu.make_async_copy(
+                other.at[rows, pl.ds(begin, lanes)],
+                right.at[slot, :, pl.ds(0, lanes)],
+                rsem.at[slot],
+            ),
+        )
+
+    def place_of(entry, step):
+        return lax.rem(entry * steps + step, SLOTS)
+
     def multiply(number):
-        kind, place, parts, _, _ = chunks[number]
-        for one, other, begin, at, lanes in parts:
-            height = one.shape[1]
-
-            def load(step, slot):
-                rows = pl.ds(pl.multiple_of(step * STEP, STEP), STEP)
-                return (
-                    pltpu.make_async_copy(
-                        one.at[rows, :], left.at[slot, :, pl.ds(0, height)], lsem.at[slot]
-                    ),
-                    pltpu.make_async_copy(
-                        other.at[rows, pl.ds(begin, lanes)],
-                        right.at[slot, :, pl.ds(0, lanes)],
-                        rsem.at[slot],
-                    ),
-                )
-
-            for copy in load(0, 0):
-                copy.start()
-            steps = tokens // STEP
+        kind, place = chunks[number][:2]
+        for entry in range(begins[number], begins[number + 1]):
+            at, lanes = line_up[entry][3:5]
 
             def body(step, carry):
-                slot = lax.rem(step, 2)
-
-                @pl.when(step + 1 < steps)
+                ahead = step + SLOTS - 1
+
+                @pl.when(ahead < steps)
                 def _():
-                    for copy in load(step + 1, lax.rem(step + 1, 2)):
+                    for copy in load(entry, ahead, place_of(entry, ahead)):
                         copy.start()
 
-                for copy in load(step, slot):
+                if entry + 1 < len(line_up):
+
+                    @pl.when(ahead >= steps)
+                    def _():
+                        for copy in load(entry + 1, ahead - steps, place_of(entry, ahead)):
+                            copy.start()
+
+                slot = place_of(entry, step)
+                for copy in load(entry, step, slot):
                     copy.wait()
-                for group in range(height // width):
-                    rows = slice(group * width, (group + 1) * width)
-                    columns = slice(at + group * lanes, at + (group + 1) * lanes)
-                    product = dot(left[slot, :, rows], right[slot, :, :lanes], 0, 0)
-
-                    @pl.when(step == 0)
-                    def _():
-                        total[:, columns] = product
-
-                    @pl.when(step > 0)
-                    def _():
-                        total[:, columns] += product
+                product = dot(left[slot], right[slot, :, :lanes], 0, 0)
+                columns = slice(at, at + lanes)
+
+                @pl.when(step == 0)
+                def _():
+                    total[:, columns] = product
+
+                @pl.when(step > 0)
+                def _():
+                    total[:, columns] += product
 
                 return carry
 
@@ -691,11 +708,17 @@
     for step in range(len(masks))[::-1]:
         stages.append(functools.partial(line_add, step=step))
 
+    for step in range(SLOTS - 1):
+        for copy in load(0, step, step):
+            copy.start()
     second = None
-    for turn in range(len(chunks) + len(stages) - 1):
+    lags = [0, 1, 3]
+    while len(lags) < len(stages):
+        lags.append(lags[-1] + 1)
+    for turn in range(len(chunks) + lags[-1]):
         for depth in range(len(stages))[::-1]:
-            if depth > 0 and 0 <= turn - depth < len(chunks):
-                stages[depth](turn - depth)
+            if depth > 0 and 0 <= turn - lags[depth] < len(chunks):
+                stages[depth](turn - lags[depth])
         if turn < len(chunks):
             multiply(turn)
             core_start(turn)
@@ -749,12 +772,12 @@
             VMEM((2, frames, rows_d, narrow), bf16),
             VMEM((6, frames - 1, rows_w, wide), bf16),
             VMEM((2, frames - 1, rows_d, narrow), bf16),
-            VMEM((2, STEP, hidden), bf16),
-            VMEM((2, STEP, wide), bf16),
+            VMEM((SLOTS, STEP, width), bf16),
+            VMEM((SLOTS, STEP, wide), bf16),
             VMEM((width, wide), f32),
             VMEM((frames,) + small.shape, f32),
             VMEM(small.shape, f32),
-            DMA((2,)), DMA((2,)),
+            DMA((SLOTS,)), DMA((SLOTS,)),
             DMA((8, clips // 2)), DMA((8, clips // 2)),
             DMA((8, 2, peers)), DMA((8, 2, peers)),
             DMA((8, frames - 1)), DMA((8, frames - 1)),
@@ -848,27 +871,163 @@
 
 
 def middle_kernel(
-    clip, after_ref, cot_ref, loss, mod, w_b, w_u, w_d,
-    out_ref, grad_ref, act_ref, gup_ref, h3_ref, gb3_ref, mixed_ref, gb2_ref, h2_ref, gqkv_ref, sums,
-    qkv, totals, mask, gmix,
+    clips, frames, tiles,
+    after_first, cot_first, after_later, cotangent, loss, mod, w_b, w_u, w_d,
+    act_ref, gup_ref, h3_ref, gb3_ref, mixed_ref, gb2_ref, h2_ref, gqkv_ref, sums,
+    after_second, cot_second, grad_first, out_first, grad_later, out_later,
+    qkv, totals, mask, gmix, after_tile, cot_tile, grad_stage, out_stage,
+    ts, tr, us, ur, gs, gr, os, orr, ls, ks, ws,
 ):
-    width = after_ref.shape[-1]
-    group = after_ref.shape[2]
-    tokens = after_ref.shape[0] * after_ref.shape[1] * group
+    frame = lax.axis_index("frame")
+    step = pl.program_id(0)
+    last = pl.num_programs(0) - 1
+    clip = lax.div(step, tiles)
+    tile = lax.rem(step, tiles)
+    slot = lax.rem(step, 2)
+    width = mod.shape[1]
+    frame_count, group = after_tile.shape[2], after_tile.shape[3]
+    part = tiles * group
+    tokens = frames * frame_count * group
     row = clip * 9
-    piece = lambda number: mod[row + number : row + number + 1, :]
-
-    @pl.when(pl.program_id(0) == 0)
+    piece = lambda number: mod[pl.ds(row + number, 1), :]
+
+    def own_part(index):
+        return pl.ds(pl.multiple_of(index * part, part), part)
+
+    def later_copies():
+        copies = []
+        for hop in range(1, frames):
+            peer = lax.rem(frame + hop, frames)
+            for source, target, send, recv in (
+                (after_later.at[:, own_part(peer), :], after_second, ts, tr),
+                (cotangent.at[1, :, own_part(peer), :], cot_second, us, ur),
+            ):
+                copies.append(
+                    pltpu.make_async_remote_copy(
+                        src_ref=source,
+                        dst_ref=target.at[frame],
+                        send_sem=send.at[hop - 1],
+                        recv_sem=recv.at[hop - 1],
+                        device_id={"frame": peer},
+                        device_id_type=MESH,
+                    )
+                )
+        return copies[0::2] + copies[1::2]
+
+    def own_copies():
+        return (
+            pltpu.make_async_copy(
+                after_later.at[:, own_part(frame), :], after_second.at[frame], ks.at[0]
+            ),
+            pltpu.make_async_copy(
+                cotangent.at[1, :, own_part(frame), :], cot_second.at[frame], ks.at[1]
+            ),
+        )
+
+    def load(source, other, index, place):
+        rows = pl.ds(pl.multiple_of(index * group, group), group)
+        return (
+            pltpu.make_async_copy(source.at[:, :, rows, :], after_tile.at[place], ls.at[place, 0]),
+            pltpu.make_async_copy(other.at[:, :, rows, :], cot_tile.at[place], ls.at[place, 1]),
+        )
+
+    def tile_copies(index):
+        rows = pl.ds(pl.multiple_of(index * group, group), group)
+        far = pl.ds(pl.multiple_of(frame * part + index * group, group), group)
+        copies = []
+        for hop in range(1, frames):
+            peer = lax.rem(frame + hop, frames)
+            for source, target, send, recv in (
+                (grad_stage, grad_first.at[frame, :, rows, :], gs, gr),
+                (out_stage, out_first.at[:, far, :], os, orr),
+            ):
+                copies.append(
+                    pltpu.make_async_remote_copy(
+                        src_ref=source.at[index, peer],
+                        dst_ref=target,
+                        send_sem=send.at[index, hop - 1],
+                        recv_sem=recv.at[index, hop - 1],
+                        device_id={"frame": peer},
+                        device_id_type=MESH,
+                    )
+                )
+        return copies
+
+    def tile_own(index):
+        rows = pl.ds(pl.multiple_of(index * group, group), group)
+        far = pl.ds(pl.multiple_of(frame * part + index * group, group), group)
+        return (
+            pltpu.make_async_copy(
+                grad_stage.at[index, frame], grad_first.at[frame, :, rows, :], ws.at[0, index]
+            ),
+            pltpu.make_async_copy(
+                out_stage.at[index, frame], out_first.at[:, far, :], ws.at[1, index]
+            ),
+        )
+
+    def tile_later(index):
+        place = index + tiles
+        rows = pl.ds(pl.multiple_of(index * group, group), group)
+        return (
+            pltpu.make_async_copy(
+                grad_stage.at[place], grad_later.at[:, :, rows, :], ws.at[0, place]
+            ),
+            pltpu.make_async_copy(
+                out_stage.at[place], out_later.at[:, :, rows, :], ws.at[1, place]
+            ),
+        )
+
+    @pl.when(step == 0)
     def _():
-        sums[...] = jnp.zeros_like(sums)
+        barrier = pltpu.get_barrier_semaphore()
+        for hop in range(1, frames):
+            pl.semaphore_signal(
+                barrier,
+                inc=1,
+                device_id={"frame": lax.rem(frame + hop, frames)},
+                device_id_type=MESH,
+            )
+        pl.semaphore_wait(barrier, frames - 1)
+        for copy in load(after_first, cot_first, 0, 0):
+            copy.start()
+        for copy in later_copies():
+            copy.start()
+        for copy in own_copies():
+            copy.start()
         first = lax.broadcasted_iota(jnp.int32, (tokens, tokens), 0)
         second = lax.broadcasted_iota(jnp.int32, (tokens, tokens), 1)
         mask[...] = jnp.where(lax.rem(first, group) == lax.rem(second, group), 0.0, -1e30)
 
+    @pl.when(step == tiles)
+    def _():
+        for copy in later_copies():
+            copy.wait_recv()
+        for copy in own_copies():
+            copy.wait()
+        for copy in load(after_second, cot_second, 0, slot):
+            copy.start()
+
+    for copy in load(after_first, cot_first, 0, slot):
+        copy.wait()
+
+    @pl.when(step + 1 < tiles)
+    def _():
+        for copy in load(after_first, cot_first, step + 1, 1 - slot):
+            copy.start()
+
+    @pl.when((step >= tiles) & (step < last))
+    def _():
+        for copy in load(after_second, cot_second, tile + 1, 1 - slot):
+            copy.start()
+
+    @pl.when(tile == 0)
+    def _():
+        sums[...] = jnp.zeros_like(sums)
+
     def add(place, values):
         sums[place : place + 1, :] += values
 
-    after = after_ref[...].reshape(tokens, width).astype(f32)
+    after = after_tile[slot].reshape(tokens, width).astype(f32)
     norm, scale = normed(after)
     hidden = (norm * (1.0 + piece(4)) + piece(3)).astype(bf16)
     h2_ref[...] = hidden
@@ -879,15 +1038,15 @@
     norm_three, scale_three = normed(after_two)
     hidden = (norm_three * (1.0 + piece(7)) + piece(6)).astype(bf16)
     h3_ref[...] = hidden
-    grad_out = cot_ref[...].reshape(tokens, width).astype(f32) * loss[clip : clip + 1, :]
+    grad_out = cot_tile[slot].reshape(tokens, width).astype(f32) * loss[pl.ds(clip, 1), :]
     grad_branch = (grad_out * piece(8)).astype(bf16)
     gb3_ref[...] = grad_branch
     add(11, column_sum(grad_branch.astype(f32)))
     branch_three = jnp.zeros((tokens, width), f32)
     grad_hidden = jnp.zeros((tokens, width), f32)
     for chunk in range(w_u.shape[1] // width):
-        part = slice(chunk * width, (chunk + 1) * width)
-        upper = dot(hidden, w_u[:, part], 1, 0) + mod[20 + chunk : 21 + chunk, :]
+        cut = slice(chunk * width, (chunk + 1) * width)
+        upper = dot(hidden, w_u[:, cut], 1, 0) + mod[20 + chunk : 21 + chunk, :]
         square = upper * upper
         bend = jnp.tanh(upper * (GELU_C + (GELU_C * GELU_A) * square))
         half = 0.5 + 0.5 * bend
@@ -895,15 +1054,15 @@
         slope = half + (0.5 * upper) * (1.0 - bend * bend) * (
             GELU_C + (3.0 * GELU_C * GELU_A) * square
         )
-        act_ref[:, part] = act
-        branch_three += dot(act, w_d[part, :], 1, 0)
-        grad_upper = (dot(grad_branch, w_d[part, :], 1, 1) * slope).astype(bf16)
-        gup_ref[:, part] = grad_upper
+        act_ref[:, cut] = act
+        branch_three += dot(act, w_d[cut, :], 1, 0)
+        grad_upper = (dot(grad_branch, w_d[cut, :], 1, 1) * slope).astype(bf16)
+        gup_ref[:, cut] = grad_upper
         add(7 + chunk, column_sum(grad_upper.astype(f32)))
-        grad_hidden += dot(grad_upper, w_u[:, part], 1, 1)
+        grad_hidden += dot(grad_upper, w_u[:, cut], 1, 1)
     branch_three += mod[24:25, :]
     out = (after_two + piece(8) * branch_three).astype(bf16)
-    out_ref[...] = out.reshape(out_ref.shape)
+    out_stage[step] = out.reshape(out_stage.shape[1:])
     add(5, column_sum(grad_out * branch_three))
     add(3, column_sum(grad_hidden))
     add(4, column_sum(grad_hidden * norm_three))
@@ -918,58 +1077,86 @@
     add(0, column_sum(grad_hidden))
     add(1, column_sum(grad_hidden * norm))
     grad_one = grad_two + norm_back(grad_hidden, 1.0 + piece(4), norm, scale)
-    grad_ref[...] = grad_one.astype(bf16).reshape(grad_ref.shape)
-
-
-def middle_kernel_next(count, clip, *refs):
-    middle_kernel(clip, *refs[:7], *refs[7 + count :])
-
-
-def middle_call(clip, clip_count, after, cot, loss, mod, w_b, w_u, w_d, earlier):
-    frames, frame_count, part, width = after.shape
+    grad_stage[step] = grad_one.astype(bf16).reshape(grad_stage.shape[1:])
+
+    @pl.when(step < tiles)
+    def _():
+        for copy in tile_copies(tile):
+            copy.start()
+        for copy in tile_own(tile):
+            copy.start()
+
+    @pl.when(step >= tiles)
+    def _():
+        for copy in tile_later(tile):
+            copy.start()
+
+    @pl.when(step == last)
+    def _():
+        for copy in later_copies():
+            copy.wait_send()
+
+        def settle(index, carry):
+            for copy in tile_copies(index):
+                copy.wait_send()
+                copy.wait_recv()
+            for copy in tile_own(index) + tile_later(index):
+                copy.wait()
+            return carry
+
+        lax.fori_loop(0, tiles, settle, 0)
+
+
+def middle_call(
+    clips, frames, after_first, cot_first, after_later, cotangent, loss, mod, w_b, w_u, w_d
+):
+    _, frame_count, part, width = after_first.shape
     group = min(16, part)
     tiles = part // group
     tokens = frames * frame_count * group
     hidden_width = w_u.shape[1]
-    block = pl.BlockSpec((frames, frame_count, group, width), lambda t: (0, 0, t, 0))
     widths = (hidden_width, hidden_width, width, width, width, width, width, 3 * width)
-    own = lambda columns: pl.BlockSpec((tokens, columns), lambda t: (clip * tiles + t, 0))
-    rows = tiles * tokens
-    in_specs = [
-        block, block, full(loss.shape), full(mod.shape), full(w_b.shape), full(w_u.shape),
-        full(w_d.shape),
-    ]
-    args = [after, cot, loss, mod, w_b, w_u, w_d]
-    body = functools.partial(middle_kernel, clip)
-    aliases = {}
-    if earlier is not None:
-        in_specs += [pl.BlockSpec(memory_space=pl.ANY)] * len(earlier)
-        args += list(earlier)
-        aliases = {7 + number: 2 + number for number in range(len(earlier))}
-        body = functools.partial(middle_kernel_next, len(earlier), clip)
+    own = lambda columns: pl.BlockSpec((tokens, columns), lambda t: (t, 0))
+    hbm = pl.BlockSpec(memory_space=pl.ANY)
+    rows = 2 * tiles * tokens
+    traded = jax.ShapeDtypeStruct(after_first.shape, bf16)
+    slab = (frames, frame_count, group, width)
     return pl.pallas_call(
-        body,
-        grid=(tiles,),
-        in_specs=in_specs,
-        out_specs=[block, block] + [own(columns) for columns in widths]
-        + [pl.BlockSpec((16, width), lambda t: (0, 0))],
-        out_shape=[
-            jax.ShapeDtypeStruct(after.shape, bf16), jax.ShapeDtypeStruct(after.shape, bf16),
-        ]
-        + [jax.ShapeDtypeStruct((clip_count * rows, columns), bf16) for columns in widths]
-        + [jax.ShapeDtypeStruct((16, width), f32)],
+        functools.partial(middle_kernel, clips, frames, tiles),
+        grid=(2 * tiles,),
+        in_specs=[
+            hbm, hbm, hbm, hbm, full(loss.shape), full(mod.shape), full(w_b.shape),
+            full(w_u.shape), full(w_d.shape),
+        ],
+        out_specs=[own(columns) for columns in widths]
+        + [pl.BlockSpec((None, 16, width), lambda t: (t // tiles, 0, 0))]
+        + [hbm] * 6,
+        out_shape=[jax.ShapeDtypeStruct((rows, columns), bf16) for columns in widths]
+        + [
+            jax.ShapeDtypeStruct((2, 16, width), f32),
+            traded, traded, traded,
+            jax.ShapeDtypeStruct((frame_count, frames * part, width), bf16),
+            traded, traded,
+        ],
         scratch_shapes=[
             VMEM((tokens, 3 * width), bf16),
             VMEM((16, tokens), f32),
             VMEM((tokens, tokens), f32),
             VMEM((tokens, width), bf16),
+            VMEM((2,) + slab, bf16),
+            VMEM((2,) + slab, bf16),
+            VMEM((2 * tiles,) + slab, bf16),
+            VMEM((2 * tiles,) + slab, bf16),
+            DMA((frames - 1,)), DMA((frames - 1,)),
+            DMA((frames - 1,)), DMA((frames - 1,)),
+            DMA((tiles, frames - 1)), DMA((tiles, frames - 1)),
+            DMA((tiles, frames - 1)), DMA((tiles, frames - 1)),
+            DMA((2, 2)), DMA((2,)), DMA((2, 2 * tiles)),
         ],
-        input_output_aliases=aliases,
-        compiler_params=pltpu.CompilerParams(vmem_limit_bytes=VMEM_LIMIT),
-        cost_estimate=pl.CostEstimate(
-            flops=rows * 100_000_000, bytes_accessed=rows * 40_000, transcendentals=0
+        compiler_params=pltpu.CompilerParams(
+            collective_id=2, has_side_effects=True, vmem_limit_bytes=VMEM_LIMIT
         ),
-    )(*args)
+    )(after_first, cot_first, after_later, cotangent, loss, mod, w_b, w_u, w_d)
 
 
 def space_back_kernel(
@@ -1102,26 +1289,14 @@
 
     loss = jnp.exp2(weight_index.astype(f32) * 0.5 - 1.0)
     loss = jnp.broadcast_to(loss[:, None], (clip_count, width))
-    cots, afters = [cot_first], [after_first]
-    for clip in range(1, clip_count):
-        patches = cotangent[clip].reshape(frame_count, frames, part, width)
-        cots.append(exchange(jnp.swapaxes(patches, 0, 1)))
-        place = (clip - 1) * frame_count
-        patches = after_later[place : place + frame_count]
-        patches = patches.reshape(frame_count, frames, part, width)
-        afters.append(exchange(jnp.swapaxes(patches, 0, 1)))
-
-    earlier = None
-    outs, grads, mid_sums = [], [], []
-    for clip in range(clip_count):
-        out, grad, *rest = middle_call(
-            clip, clip_count, afters[clip], cots[clip], loss, mod, w_b, w_u, w_d, earlier
-        )
-        earlier = rest[:-1]
-        mid_sums.append(rest[-1])
-        outs.append(exchange(out))
-        grads.append(exchange(grad))
-    act, gup, h3, gb3, mixed_two, gb2, h2, gqkv_two = earlier
+    (
+        act, gup, h3, gb3, mixed_two, gb2, h2, gqkv_two, mid_sums, _, _, grad_first, out_first,
+        grad_later, out_later,
+    ) = middle_call(
+        clips, frames, after_first, cot_first, after_later, cotangent, loss, mod, w_b, w_u, w_d
+    )
+    grads = [grad_first, exchange(grad_later)]
+    out_second = jnp.swapaxes(exchange(out_later), 0, 1).reshape(out_first.shape)
 
     earlier = None
     space_sums = []
@@ -1156,12 +1331,7 @@
         length = vector.shape[0] // owners
         return lax.dynamic_slice_in_dim(vector, owner * length, length, 0)
 
-    outputs = jnp.stack(
-        [
-            jnp.swapaxes(out, 0, 1).reshape(frame_count, patch_count, width)
-            for out in outs
-        ]
-    )
+    outputs = jnp.stack([out_first, out_second])
     return (
         outputs,
         input_grad,

time: 661 us -> 560 us (0.85)
  blocking collectives: 41 us -> 0 us
  waiting for transfers between devices: 38.2 us -> 1.18 us
  Pallas kernels: 506 us -> 480 us
  starting transfers between devices: 19.4 us -> 31 us
  local copies, waits for them, and re-layouts: 29.9 us -> 22.7 us
    all_to_all x1 -> x0, blocking collectives: 41 us -> none  [exchange(): lax.all_to_all(values, 'frame', split_axis=0, concat_axis=0, tiled=True)]
    all_to_all x5 -> x2, waiting for transfers between devices: 38.2 us -> 1.18 us  [exchange(): lax.all_to_all(values, 'frame', split_axis=0, concat_axis=0, tiled=True)]
    pallas_call x1, Pallas kernels: 171 us -> 134 us  [grad_call(): pl.pallas_call(functools.partial(grad_kernel, clips, frames), out_shape=(...]
    all_to_all x5 -> x2, starting transfers between devices: 19.4 us -> 31 us  [exchange(): lax.all_to_all(values, 'frame', split_axis=0, concat_axis=0, tiled=True)]
    pallas_call x2 -> x1, Pallas kernels: 147 us -> 158 us  [middle_call(): pl.pallas_call(functools.partial(middle_kernel, clips, frames, tiles), gr...]
  transfers between devices with their start and end apart: 5 -> 2, of which waited for: 2 -> 1; matrix products, arithmetic and copies ran while one was open for 2% -> 2% of each run, Pallas kernels for 59% -> 36%
where the time goes in v3:
time: 560 us; the launch traced here: 551 us
  Pallas kernels  480 us (86%)
  starting transfers between devices  31 us (6%)
  local copies, waits for them, and re-layouts  22.7 us (4%)
  other arithmetic  14.3 us (3%)
    pallas_call x1, Pallas kernels, middle_call(): pl.pallas_call(functools.partial(middle_kernel, clips, frames, tiles), gr...  158 us
    pallas_call x1, Pallas kernels, grad_call(): pl.pallas_call(functools.partial(grad_kernel, clips, frames), out_shape=(...  134 us
    pallas_call x1, Pallas kernels, start_call(): pl.pallas_call(functools.partial(start_kernel, clips, frames, clip_count)...  124 us
    pallas_call x2, Pallas kernels, space_back_call(): pl.pallas_call(body, grid=(frame_count,), in_specs=in_specs, out_specs=[p...  63.5 us
    all_to_all x2, starting transfers between devices, exchange(): lax.all_to_all(values, 'frame', split_axis=0, concat_axis=0, tiled=True)  31 us
  transfers between devices with their start and end apart: 2, of which 1 were waited for; matrix products, arithmetic and copies ran while one was open for 2% of the time, Pallas kernels for 36%

profile of v3, /device:TPU:0, one launch (start us, length us, event | category | flops | bytes accessed | tf_op | source)
XLA Modules:
  0.0 551.4 jit_solution(6680222909182297949)
XLA Ops:
  1.4 0.7 multiply_exponential_fusion.1
  4.0 0.7 convert_dynamic-update-slice_fusion.1
  4.8 0.8 convert_dynamic-update-slice_fusion
  6.3 2.3 pad.13.ada
  9.1 1.6 pad_maximum_fusion.1.sh_c
  10.7 1.6 pad_maximum_fusion.2.sh_b
  12.2 0.8 fusion.1.select
  13.1 2.0 concatenate.18.bias
  15.1 124.4 %shard_map.263 = (bf16[768,3072]{1,0:T(8,128)(2,1)}, bf16[768,3072]{1,0:T(8,128)(2,1)}, bf16[768,3072]{1,0:T(8,128)(2,1)}, bf16[3072,768]{1,0:T(8,128)(2,1)}, f3...) custom-call(bf16[2,4,256,768]{3,2,1,0:T(8,128)(2,1)} %refs_1_.1, ...), custom_call_target="tpu_custom_call" | custom-call | tf_op jit(solution)/shard_map/pallas_call | solution.py:440
  139.5 0.7 broadcast_in_dim.16.loss
  140.2 157.9 %shard_map.264 = (bf16[2048,3072]{1,0:T(8,128)(2,1)}, bf16[2048,3072]{1,0:T(8,128)(2,1)}, bf16[2048,768]{1,0:T(8,128)(2,1)}, bf16[2048,768]{1,0:T(8,128)(2,1)}, ...) custom-call(bf16[4,4,64,768]{3,2,1,0:T(8,128)(2,1)} %get-tuple-eleme, ...), custom_call_target="tpu_custom_call" | custom-call | tf_op jit(solution)/shard_map/pallas_call | solution.py:1124
  298.1 27.1 %all-to-all-start.1 = ((bf16[4,4,64,768]{3,2,1,0:T(8,128)(2,1)}), bf16[4,4,64,768]{3,2,1,0:T(8,128)(2,1)S(1)}, u32[]{:S(2)}, u32[]{:S(2)}) async-start(bf16[4,4,64,768]{3,2,1,0:T(8,128)(2,1)} %get-tuple-element.63), calls=%async_computation.1 | async-start | bytes 3145728 | tf_op jit(solution)/shard_map/all_to_all | solution.py:1288
  325.1 0.7 slice.92
  325.8 31.7 %shard_map.265 = (f32[2,4,256,768]{3,2,1,0:T(8,128)}, bf16[2048,768]{1,0:T(8,128)(2,1)}, bf16[2048,2304]{1,0:T(8,128)(2,1)}, f32[8,768]{1,0:T(8,128)}) custom-call(bf16[4,4,64,768]{3,2,1,0:T(8,128)(2,1)} %get-tuple-element.68.grad_ref, bf16[2,4,256,768]{3,2,1,0:T(8,128)(2,1)} %refs_1_.1, f32[32,768]{1,0:T(8,128)} %get-tuple-element.57.mod.refs_2_, ...), custom_call_target="tpu_custom_call" | custom-call | flops 20480000000 | bytes 15728640 | tf_op jit(solution)/shard_map/pallas_call | solution.py:1220
  357.6 0.7 slice.72
  358.3 1.2 all-to-all-done.1.refs_0_
  359.5 3.9 all-to-all-start
  363.4 31.7 %shard_map.266 = (f32[2,4,256,768]{3,2,1,0:T(8,128)}, bf16[2048,768]{1,0:T(8,128)(2,1)}, bf16[2048,2304]{1,0:T(8,128)(2,1)}, f32[8,768]{1,0:T(8,128)}) custom-call(bf16[4,4,64,768]{3,2,1,0:T(8,128)(2,1)} %copy-done, bf16[2,4,256,768]{3,2,1,0:T(8,128)(2,1)} %refs_1_.1, ...), custom_call_target="tpu_custom_call", output_to_operand_aliasing={{0}: (7, {}), {1}: (8, {}), {2}: (9, {})} | custom-call | flops 20480000000 | bytes 15728640 | tf_op jit(solution)/shard_map/pallas_call | solution.py:1220
  395.2 0.7 slice.75
  395.9 0.8 slice_add_fusion
  397.7 134.1 %shard_map.267 = (f32[8,32,768]{2,1,0:T(8,128)}, f32[24,3072]{1,0:T(8,128)}, f32[96,768]{1,0:T(8,128)}, f32[24,3072]{1,0:T(8,128)}, f32[24,3072]{1,0:T(8,128)}) custom-call(f32[32,768]{1,0:T(8,128)} %pad.14.small, bf16[2048,768]{1,0:T(8,128)(2,1)} %get-tuple-element.77.h3, bf16[2048,3072]{1,0:T(8,128)(2,1)} %get-tuple-element.78.gup, ...), custom_call_target="tpu_custom_call" | custom-call | tf_op jit(solution)/shard_map/pallas_call | solution.py:753
  531.9 1.5 slice.84
  533.4 1.6 slice.83
  535.0 1.5 slice.88
  536.5 1.6 slice.87
  538.2 1.9 slice.82
  540.1 1.0 slice_reduce_fusion
  541.3 1.2 reshape.106
  544.4 1.3 fusion.7
  545.7 3.4 pad_maximum_fusion
  549.7 0.7 copy.46
  550.5 0.7 copy.47
  (41 shorter events, 7.5 us)
Async XLA Ops:
  298.1 61.4 %all-to-all-start.1 = ((bf16[4,4,64,768]{3,2,1,0:T(8,128)(2,1)}), bf16[4,4,64,768]{3,2,1,0:T(8,128)(2,1)S(1)}, u32[]{:S(2)}, u32[]{:S(2)}) async-start(bf16[4,4,64,768]{3,2,1,0:T(8,128)(2,1)} %get-tuple-element.63), calls=%async_computation.1 | async-start | bytes 3145728 | tf_op jit(solution)/shard_map/all_to_all | solution.py:1288
  325.8 32.5 %copy-start.3 = (f32[2,16,768]{2,1,0:T(8,128)S(1)}, f32[2,16,768]{2,1,0:T(8,128)}, u32[]{:S(2)}) copy-start(f32[2,16,768]{2,1,0:T(8,128)} %get-tuple-element.75) | copy-start | bytes 294916
  359.5 3.9 copy-start
  359.5 181.7 %all-to-all-start = ((bf16[4,4,64,768]{3,2,1,0:T(8,128)(2,1)}), bf16[4,4,64,768]{3,2,1,0:T(8,128)(2,1)S(1)}, u32[]{:S(2)}, u32[]{:S(2)}) async-start(bf16[4,4,64,768]{3,2,1,0:T(8,128)(2,1)} %get-tuple-element.62), calls=%async_computation | async-start | bytes 3145728 | tf_op jit(solution)/shard_map/all_to_all | solution.py:1288
  545.7 4.0 copy-start.2
  545.7 4.7 copy-start.1
